TPU v7x, 32 devices: a whole 2x2x4 slice. The times are simulated.
32 devices in a mesh: ha: 8 (over z, y), ta: 2 (over x), col: 2 (over core).
Axes of the slice: x: 2, y: 2, z: 4, core: 2. Of those that a mesh axis runs over, the one named last changes fastest.
Arguments:
- tokens: bfloat16 [16, 224, 28, 128], P(('col', 'ta'), 'ha'), parts along dimension 0, may hold values from -6 to 6
- regions_one: int32 [16, 224, 28], P(('col', 'ta'), 'ha'), parts along dimension 0, may hold values from 0 to 2
- regions_three: int32 [16, 56, 7], P(('col', 'ta'), 'ha'), parts along dimension 0, may hold values from 0 to 2
- gain_one: float32 [128], replicated, may hold values from 0.25 to 1.75
- projection_one: bfloat16 [128, 384], replicated, may hold values from -0.5 to 0.5
- outward_one: bfloat16 [128, 128], replicated, may hold values from -0.5 to 0.5
- table_one: float32 [1183, 4], replicated, may hold values from -4 to 303
- merge_gain_one: float32 [512], replicated, may hold values from 0.25 to 1.75
- merge_weight_one: bfloat16 [512, 256], replicated, may hold values from -0.25 to 0.25
- merge_gain_two: float32 [1024], replicated, may hold values from 0.25 to 1.75
- merge_weight_two: bfloat16 [1024, 512], replicated, may hold values from -0.1875 to 0.1875
- gain_three: float32 [512], replicated, may hold values from 0.25 to 1.75
- projection_three: bfloat16 [512, 1536], replicated, may hold values from -0.25 to 0.25
- outward_three: bfloat16 [512, 512], replicated, may hold values from -0.25 to 0.25
- table_three: float32 [1183, 16], replicated, may hold values from -4 to 303
- cotangent: bfloat16 [16, 56, 7, 512], P(('col', 'ta'), 'ha'), parts along dimension 0, may hold values from -6 to 6
Outputs:
- section_three: bfloat16 [16, 56, 7, 512], P(('col', 'ta'), 'ha'), parts along dimension 0
- grad_tokens: bfloat16 [16, 224, 28, 128], P(('col', 'ta'), 'ha'), parts along dimension 0
There are 2 independent parts, one for each index of `col`. A program takes and returns all parts, laid end to end along the dimension named above; an argument that names none is the same for every part. Nothing has to cross between parts.
Inputs may be any that keep to these rules, and one draw needn't show every extreme that they name: `regions_one`: region ids are free for each position. `regions_three`: region ids are free for each position.
All inputs are finite; a program needn't handle non-finite values.
Results may differ from a plain program's by a relative error of at most 0.03.
Values may be sent and summed in bfloat16 or wider, within the bound.
No kernel may reach another device: no remote copies, remote signals or barrier semaphores. Data moves between devices by JAX's collectives and lax.ppermute only.
A program may use at most 192 MiB of HBM per device.

v0:
```python
import functools

import jax
import jax.numpy as jnp
import numpy as np
from jax import lax
from jax.experimental import pallas as pl
from jax.experimental.layout import Layout, with_layout_constraint
from jax.experimental.pallas import tpu as pltpu
from jax.sharding import PartitionSpec as P

HEADS1 = 4
HEADS3 = 16
WT = 4
WS = 7
ST = 2
SS = 3
EPSILON = 1e-05
NREL = 1183
LOG2E = 1.4426950408889634
HEAD = 32
SCALE = HEAD**-0.5
ROWS = WT * WS * 8
LANES = 256
SPAN = 1280
GONE = -1e30
PER_STEP = 8
STEPS = 8 // PER_STEP
BF = jnp.bfloat16
F32 = jnp.float32


def dot(a, b):
    return jnp.dot(a, b, preferred_element_type=F32)


def dot_nt(a, b):
    return lax.dot_general(a, b, (((1,), (1,)), ((), ())), preferred_element_type=F32)


def params(limit=20):
    return pltpu.CompilerParams(vmem_limit_bytes=limit * 1024 * 1024)


def cost(us):
    return pl.CostEstimate(flops=int(us * 1.1e9), bytes_accessed=int(us * 1e6), transcendentals=0)


def normalise(x):
    centred = x - jnp.mean(x, -1, keepdims=True)
    rstd = lax.rsqrt(jnp.mean(centred * centred, -1, keepdims=True) + EPSILON)
    return centred * rstd, rstd


def normalise_back(grad, xhat, rstd):
    return rstd * (
        grad
        - jnp.mean(grad, -1, keepdims=True)
        - xhat * jnp.mean(grad * xhat, -1, keepdims=True)
    )


def head_rows(x, h):
    return x[HEAD * h : HEAD * (h + 1)]


def head_of_lane(shape):
    return lax.broadcasted_iota(jnp.int32, shape, 1) // HEAD


def by_head(x):
    lane = head_of_lane((1, 128))
    return jnp.concatenate([x * (lane == h).astype(F32).astype(BF) for h in range(4)], 0)


def pick_heads(stacked):
    lane = head_of_lane((ROWS, 128))
    got = stacked[:ROWS]
    for h in range(1, 4):
        got = jnp.where(lane == h, stacked[ROWS * h : ROWS * (h + 1)], got)
    return got


def lengthen(x):
    return jnp.concatenate([x, jnp.zeros((LANES - ROWS, x.shape[1]), x.dtype)], 0)


def region_mask(column, row):
    return jnp.where(jnp.concatenate([column, column], 1) == row, 0.0, GONE).astype(F32)


def stagger(pending):
    pending, active = list(pending), []
    while pending or active:
        if pending:
            active.append(pending.pop(0))
        active = [g for g in active if next(g, "end") is None]


def attend_four(windows, beside=()):
    scores = [dot(by_head(k), qT) for k, qT, _, _, _, _ in windows]
    results = []
    beside = list(beside)
    share = -(-len(beside) // len(windows))
    for s, (_, _, vT, mask, bias_at, keep_probs) in zip(scores, windows):
        for emit in beside[:share]:
            emit()
        beside = beside[share:]
        outs, inverses = [], []
        for h in range(4):
            biased = s[ROWS * h : ROWS * (h + 1)] + (bias_at(h) + mask)
            peak = jnp.max(biased, 0, keepdims=True)
            probs = jnp.exp2(biased - peak).astype(BF)
            keep_probs(h, probs)
            extended = jnp.concatenate([head_rows(vT, h)[:, :ROWS], jnp.ones((16, ROWS), BF)], 0)
            out = dot(extended, probs)
            inverse = 1.0 / out[HEAD : HEAD + 1]
            outs.append(out[:HEAD] * inverse)
            inverses.append(inverse)
        results.append((jnp.concatenate(outs, 0), jnp.concatenate(inverses + inverses, 0)))
    return results


def attend_four_back(v, qT, kT, oT, doT, inverse, probs_at):
    scaled, deltas = [], []
    for h in range(4):
        part = head_rows(doT, h) * inverse[h : h + 1]
        deltas.append(jnp.sum(part * head_rows(oT, h), 0, keepdims=True))
        scaled.append(part)
    scaled = jnp.concatenate(scaled, 0).astype(BF)
    dprobs = dot(by_head(v), scaled)
    yield
    probs = [probs_at(h) for h in range(4)]
    dscores = [
        (probs[h].astype(F32) * (dprobs[ROWS * h : ROWS * (h + 1)] - deltas[h])).astype(BF)
        for h in range(4)
    ]
    dv = pick_heads(dot_nt(jnp.concatenate(probs, 0), scaled))
    yield
    dk = pick_heads(dot_nt(jnp.concatenate(dscores, 0), qT))
    dqT = jnp.concatenate([dot(head_rows(kT, h)[:, :ROWS], dscores[h]) for h in range(4)], 0)
    yield
    dq = (dqT * SCALE).astype(BF).T[:ROWS]
    return dq, (dk * (1.0 / LOG2E)).astype(BF), dv.astype(BF)


def lanes_of(shape):
    return lax.broadcasted_iota(jnp.int32, shape, 1)


def region_rows(ids, section):
    columns = ids.shape[1]
    count = columns // WS
    place = lax.broadcasted_iota(jnp.int32, (columns, LANES * count), 0)
    lane = lanes_of((columns, LANES * count))
    column = lane % 8
    real = (column < WS) & (lane % LANES < ROWS)
    if section == 3:
        column = jnp.where(column < 3, column + 4, column - 3)
    chosen = real & (place == lane // LANES * WS + column)
    spread = dot(ids.astype(F32).astype(BF), chosen.astype(F32).astype(BF))
    row = lax.broadcasted_iota(jnp.int32, spread.shape, 0)
    lane = lanes_of(spread.shape)
    real = (lane[:1] % 8 < WS) & (lane[:1] % LANES < ROWS)
    rows = []
    for hw in range(ids.shape[0] // (WT * WS)):
        mine = lane % LANES // 8 == row % 4 * WS + row // 4 - WS * hw
        inside = (row >= WT * WS * hw) & (row < WT * WS * (hw + 1))
        found = jnp.sum(jnp.where(mine & inside, spread, 0.0), 0, keepdims=True)
        found = jnp.where(real, found, -1.0)
        rows += [found[:, LANES * ww : LANES * (ww + 1)] for ww in range(count)]
    return rows


def region_columns(ids, section):
    columns = ids.shape[1]
    count = columns // WS
    source = ids.astype(F32).astype(BF)
    token = lax.broadcasted_iota(jnp.int32, (ROWS, ids.shape[0]), 0)
    place = lanes_of((ROWS, ids.shape[0]))
    column = lax.broadcasted_iota(jnp.int32, (ROWS, columns), 0) % 8
    lane = lanes_of((ROWS, columns))
    if section == 3:
        column = jnp.where(column < 3, column + 4, jnp.where(column == 7, 8, column - 3))
    ones = jnp.ones((columns, 128), BF)
    pad = lax.broadcasted_iota(jnp.int32, (ROWS, 128), 0) % 8 == 7
    found = []
    for hw in range(ids.shape[0] // (WT * WS)):
        chosen = place == (token // 8 % WS + WS * hw) * WT + token // 56
        picked = dot(chosen.astype(F32).astype(BF), source)
        for ww in range(count):
            mine = jnp.where(lane == WS * ww + column, picked, 0.0).astype(BF)
            found.append(jnp.where(pad, -1.0, dot(mine, ones)))
    return found


def bias_rows(spread, at, heads, tj, hj):
    lane = lanes_of((heads * 8, 128))
    p0, p1, p2, p3 = (
        pltpu.roll(
            spread[ti - tj + 3, at : at + heads * 8, :], (ti * 56 - (6 - hj) * 8) % 128, 1
        )
        for ti in range(WT)
    )
    left = jnp.where(lane < 56, p0, jnp.where(lane < 112, p1, p2))
    right = jnp.where(lane < 40, p2, p3)
    return left.reshape(heads, 8, 128), right.reshape(heads, 8, 128)


def prepare_kernel(
    t1_ref, t3_ref, s_ref, r1_ref, r3_ref, o1_ref, spread, row1_ref, row3_ref, col1_ref, col3_ref, tab
):
    tab[...] = jnp.zeros((24, SPAN), F32)
    tab[0:4, 0:NREL] = t1_ref[...] * LOG2E
    tab[8:24, 0:NREL] = t3_ref[...] * LOG2E
    slabs = []
    for dt in range(7):
        start = 169 * dt
        low = start // 128 * 128
        run = tab[:, low : low + 384]
        if start > low:
            run = pltpu.roll(run, 384 - (start - low), 1)
        slabs.append(run[:, :256])
    left = jnp.concatenate(slabs, 0)
    first = left.astype(BF)
    rest = left - first.astype(F32)
    second = rest.astype(BF)
    third = (rest - second.astype(F32)).astype(BF)
    chosen = s_ref[...]
    got = dot(first, chosen) + dot(second, chosen) + dot(third, chosen)
    lane16 = lanes_of((16, 128))
    for dt in range(7):
        for wj in range(8):
            part = got[24 * dt : 24 * dt + 24, 128 * wj : 128 * wj + 128]
            spread[dt, pl.ds(wj, 8, stride=8), :] = part[0:8]
            later = part[8:24]
            turned = jnp.where(lane16 % 8 < 3, pltpu.roll(later, 124, 1), pltpu.roll(later, 3, 1))
            spread[dt, pl.ds(64 + (7 if wj == 7 else (wj + 3) % 7), 16, stride=8), :] = turned
    for tj in range(WT):
        for hj in range(WS):
            row = (tj * WS + hj) * 8
            left, right = bias_rows(spread, 0, HEADS1, tj, hj)
            o1_ref[:, row : row + 8, 0:128] = left
            o1_ref[:, row : row + 8, 128:256] = right
    for i, found in enumerate(region_rows(r1_ref[...], 1)):
        row1_ref[i] = found
    row3_ref[...] = region_rows(r3_ref[...], 3)[0]
    for i, found in enumerate(region_columns(r1_ref[...], 1)):
        col1_ref[i] = found
    col3_ref[...] = region_columns(r3_ref[...], 3)[0]


def chooser():
    chosen = np.zeros((256, 1024), np.float32)
    for wj in range(WS):
        for dh in range(13):
            for wi in range(WS):
                chosen[dh * 13 + wi - wj + 6, wj * 128 + dh * 8 + wi] = 1.0
    return jnp.asarray(chosen, BF)


def by_height(ids):
    return jnp.transpose(ids, (1, 0, 2)).reshape(-1, ids.shape[2])


def prepare(table_one, table_three, regions_one, regions_three):
    return pl.pallas_call(
        prepare_kernel,
        out_shape=(
            jax.ShapeDtypeStruct((HEADS1, ROWS, LANES), F32),
            jax.ShapeDtypeStruct((7, 24 * 8, 128), F32),
            jax.ShapeDtypeStruct((16, 1, LANES), F32),
            jax.ShapeDtypeStruct((1, LANES), F32),
            jax.ShapeDtypeStruct((16, ROWS, 128), F32),
            jax.ShapeDtypeStruct((ROWS, 128), F32),
        ),
        scratch_shapes=[pltpu.VMEM((24, SPAN), F32)],
        compiler_params=params(),
        cost_estimate=cost(1.5),
    )(
        jnp.transpose(table_one),
        jnp.transpose(table_three),
        chooser(),
        by_height(regions_one),
        by_height(regions_three),
    )


def fold(values):
    return jnp.concatenate([values[..., 128 * g : 128 * g + 128] for g in range(4)], -2)


def unfold(values):
    return jnp.concatenate([values[..., 7 * g : 7 * g + 7, :] for g in range(4)], -1)


def early_kernel(tok_ref, early_ref):
    early_ref[...] = tok_ref[0:2, 3:17]


def late_kernel(tok_ref, cot_ref, late_ref, ha_ref, dg_ref):
    late_ref[:, 0:11] = tok_ref[0:2, 17:28]
    late_ref[:, 11:15] = fold(cot_ref[0:2, 3:7].astype(F32)).astype(BF)
    ha_ref[:, 0:3] = tok_ref[2:4, 0:3]
    ha_ref[:, 3:6] = fold(cot_ref[2:4, 0:3].astype(F32)).astype(BF)
    dg_ref[:, 0:3] = tok_ref[0:2, 0:3]
    dg_ref[:, 3:6] = fold(cot_ref[0:2, 0:3].astype(F32)).astype(BF)


def arrange(kernel, rows, *operands):
    return pl.pallas_call(
        kernel,
        out_shape=[jax.ShapeDtypeStruct((2, n, 28, 128), BF) for n in rows],
        compiler_params=params(8),
        cost_estimate=cost(0.3),
    )(*operands)


def put_rows(stage, frames, rows, values):
    values = values.astype(F32)
    stage[frames, rows, 0:28, :] = values
    stage[frames, rows, 28:36, :] = values[:, :, 0:8, :]


def cut_windows(stage, win):
    for hw in range(2):
        for ww in range(4):
            win[hw * 4 + ww] = stage[:, 7 * hw : 7 * hw + 7, 3 + 7 * ww : 11 + 7 * ww, :].reshape(
                ROWS, 128
            )


def join_windows(win, stage):
    for hw in range(2):
        for ww in range(4):
            stage[:, 7 * hw : 7 * hw + 7, 3 + 7 * ww : 11 + 7 * ww, :] = win[hw * 4 + ww].reshape(
                WT, WS, 8, 128
            )
    stage[:, :, 0:3, :] = stage[:, :, 28:31, :]


def front_kernel(late, *refs):
    n_in = 4 if late else 2
    pieces, refs = refs[:n_in], refs[n_in:]
    gain_ref, proj_ref, outw_ref, bias_ref, spread_ref, row_ref, col_ref = refs[:7]
    refs = refs[7:]
    n_out = 1 if late else 2
    outs, refs = refs[:n_out], refs[n_out:]
    b3_ref, xw_ref, kv_ref, t_ref, p_ref, o_ref, inv_ref, stage, win = refs
    own = pieces[0]
    if late:
        put_rows(stage, slice(0, 2), slice(0, 11), own[2:4, 17:28])
        put_rows(stage, slice(2, 4), slice(0, 11), pieces[1][:, 0:11])
        put_rows(stage, slice(0, 2), slice(11, 14), pieces[2][:, 0:3])
        put_rows(stage, slice(2, 4), slice(11, 14), pieces[3][:, 0:3])
    else:
        put_rows(stage, slice(0, 2), slice(0, 14), own[2:4, 3:17])
        put_rows(stage, slice(2, 4), slice(0, 14), pieces[1][...])
    cut_windows(stage, win)
    lax.fori_loop(
        0,
        STEPS,
        functools.partial(
            front_step, late, gain_ref, proj_ref, outw_ref, bias_ref, spread_ref, row_ref, col_ref,
            b3_ref, xw_ref, kv_ref, t_ref, p_ref, o_ref, inv_ref, win,
        ),
        0,
    )
    join_windows(win, stage)
    if late:
        outs[0][...] = stage[:, :, 0:28, :].astype(BF)
    else:
        outs[0][...] = stage[:, 0:9, 0:28, :].astype(BF)
        outs[1][...] = stage[:, 9:14, 0:28, :].astype(BF)


def front_step(
    late, gain_ref, proj_ref, outw_ref, bias_ref, spread_ref, row_ref, col_ref,
    b3_ref, xw_ref, kv_ref, t_ref, p_ref, o_ref, inv_ref, win, step, carry,
):
    first = 8 * late
    def block(tj, hj):
        def emit():
            left, right = bias_rows(spread_ref, 64, HEADS3, 2 * late + tj, hj)
            at = pl.ds(pl.multiple_of((tj * WS + hj) * 8, 8), 8)
            b3_ref[:, at, 0:128] = left
            b3_ref[:, at, 128:256] = right

        return emit

    count = 2 // STEPS
    blocks = [block(step * count + i, hj) for i in range(count) for hj in range(WS)]
    xs, operands = [], []
    for u in range(PER_STEP):
        w = step * PER_STEP + u
        x = win[w]
        xs.append(x)
        xw_ref[w] = x.astype(BF)
        xhat, _ = normalise(x)
        packed = dot((xhat * gain_ref[...]).astype(BF), proj_ref[...])
        q = (packed[:, :128] * (SCALE * LOG2E)).astype(BF)
        kv = packed[:, 128:].astype(BF)
        kv_ref[w] = kv
        qT, kT, vT = (lengthen(part).T for part in (q, kv[:, :128], kv[:, 128:]))
        t_ref[w, :128] = qT
        t_ref[w, 128:] = kT

        def keep(h, probs, w=w):
            p_ref[w, h] = probs

        operands.append(
            (kv[:, :128], qT, vT, region_mask(col_ref[first + w], row_ref[first + w]), lambda h: bias_ref[h], keep)
        )
    for u, (oT, inverse) in enumerate(attend_four(operands, blocks)):
        w = step * PER_STEP + u
        oT = oT.astype(BF)
        o_ref[w] = oT
        inv_ref[w] = inverse
        mixed = dot(oT.T[:ROWS], outw_ref[...]).astype(BF).astype(F32)
        win[w] = xs[u] + mixed
    return carry


SAVED = (
    ((ROWS, 128), BF),
    ((ROWS, 256), BF),
    ((256, LANES), BF),
    ((4, ROWS, LANES), BF),
    ((128, LANES), BF),
    ((8, LANES), F32),
)


def front(late, pieces, gain, proj, outw, bias, spread, row, column):
    consts = (gain, proj, outw, bias, spread)
    shapes = [(4, 14, 28, 128)] if late else [(4, 9, 28, 128), (4, 5, 28, 128)]
    out = pl.pallas_call(
        functools.partial(front_kernel, late),
        out_shape=[jax.ShapeDtypeStruct(s, BF) for s in shapes]
        + [jax.ShapeDtypeStruct((HEADS3, ROWS // 2, LANES), F32)]
        + [jax.ShapeDtypeStruct((8,) + s, d) for s, d in SAVED],
        scratch_shapes=[
            pltpu.VMEM((4, 14, 40, 128), F32),
            pltpu.VMEM((8, ROWS, 128), F32),
        ],
        compiler_params=params(),
        cost_estimate=cost(4.6),
    )(*pieces, *consts, row, column)
    return out[: len(shapes) + 1], out[len(shapes) + 1 :]


def back_kernel(late, *refs):
    n_in = 3 if late else 2
    pieces, refs = refs[:n_in], refs[n_in:]
    gain_ref, proj_ref, outw_ref = refs[:3]
    xw_ref, kv_ref, t_ref, p_ref, o_ref, inv_ref = refs[3:9]
    refs = refs[9:]
    n_out = 3 if late else 2
    outs, refs = refs[:n_out], refs[n_out:]
    stage, win = refs
    if late:
        put_rows(stage, slice(0, 4), slice(0, 14), pieces[0][...])
        outs[1][:, 11:15] = pieces[1][:, 0:4]
        outs[2][0:2, 3:6] = pieces[2][...]
        outs[2][2:4, 3:6] = pieces[1][:, 4:7]
    else:
        put_rows(stage, slice(0, 4), slice(0, 9), pieces[0][...])
        put_rows(stage, slice(0, 4), slice(9, 14), pieces[1][...])
    cut_windows(stage, win)
    lax.fori_loop(
        0,
        STEPS,
        functools.partial(
            back_step, gain_ref, proj_ref, outw_ref,
            xw_ref, kv_ref, t_ref, p_ref, o_ref, inv_ref, win,
        ),
        0,
    )
    join_windows(win, stage)
    if late:
        outs[0][...] = stage[0:2, 0:11, 0:28, :].astype(BF)
        outs[1][:, 0:11] = stage[2:4, 0:11, 0:28, :].astype(BF)
        outs[2][:, 0:3] = stage[:, 11:14, 0:28, :].astype(BF)
    else:
        outs[0][...] = stage[0:2, :, 0:28, :].astype(BF)
        outs[1][...] = stage[2:4, :, 0:28, :].astype(BF)


def back_step(
    gain_ref, proj_ref, outw_ref, xw_ref, kv_ref, t_ref, p_ref, o_ref, inv_ref, win, step, carry
):
    def window(w):
        dr = win[w]
        doT = dot_nt(outw_ref[...], lengthen(dr.astype(BF)))
        yield
        dq, dk, dv = yield from attend_four_back(
            kv_ref[w, :, 128:], t_ref[w, :128], t_ref[w, 128:], o_ref[w].astype(F32), doT,
            inv_ref[w], lambda h: p_ref[w, h],
        )
        dn = dot_nt(jnp.concatenate([dq, dk, dv], 1), proj_ref[...])
        yield
        xhat, rstd = normalise(xw_ref[w].astype(F32))
        win[w] = dr + normalise_back(dn * gain_ref[...], xhat, rstd)

    stagger(window(step * PER_STEP + u) for u in range(PER_STEP))
    return carry


def back(late, pieces, gain, proj, outw, saved):
    consts = (gain, proj, outw)
    if late:
        shapes = [(2, 11, 28, 128), (2, 15, 28, 128), (4, 6, 28, 128)]
    else:
        shapes = [(2, 14, 28, 128), (2, 14, 28, 128)]
    return pl.pallas_call(
        functools.partial(back_kernel, late),
        out_shape=[jax.ShapeDtypeStruct(s, BF) for s in shapes],
        scratch_shapes=[
            pltpu.VMEM((4, 14, 40, 128), F32),
            pltpu.VMEM((8, ROWS, 128), F32),
        ],
        compiler_params=params(),
        cost_estimate=cost(5.5),
    )(*pieces, *consts, *saved)


def merge_pairs(stage, gain_ref, weight):
    pairs = stage.shape[1]
    pieces = [
        stage[:, :, q % 2, pl.ds(q // 2, 16, stride=2), :].reshape(WT * pairs * 16, 128)
        for q in range(4)
    ]
    xhat, rstd = normalise(jnp.concatenate(pieces, 1))
    merged = dot((xhat * gain_ref[...]).astype(BF), weight).astype(BF).astype(F32)
    return merged, xhat, rstd


def merge_pairs_back(grad, xhat, rstd, gain_ref, weight, stage):
    pairs = stage.shape[1]
    dn = dot_nt(grad.astype(BF), weight)
    dg = normalise_back(dn * gain_ref[...], xhat, rstd)
    for q in range(4):
        stage[:, :, q % 2, pl.ds(q // 2, 16, stride=2), :] = dg[
            :, 128 * q : 128 * q + 128
        ].reshape(WT, pairs, 16, 128)


def put_pair_row(stage, at, values):
    stage[:, at // 2, at % 2, 0:28, :] = values.astype(F32)


def clear_pads(stage):
    stage[:, :, :, 28:32, :] = jnp.zeros((WT, stage.shape[1], 2, 4, 128), F32)


def pair_row(stage, at):
    return stage[:, at // 2, at % 2, 0:28, :].astype(BF)


def fold_merged(merged, pairs):
    halves = [
        merged[:, 128 * i : 128 * i + 128].reshape(WT, pairs, 16, 128)[:, :, 0:14] for i in range(2)
    ]
    return jnp.concatenate(halves, 2)


def unfold_merged(folded):
    pad = jnp.zeros(folded.shape[:2] + (2, 128), F32)
    halves = [
        jnp.concatenate([folded[:, :, 14 * i : 14 * i + 14], pad], 2).reshape(-1, 128)
        for i in range(2)
    ]
    return jnp.concatenate(halves, 1)


def send_kernel(res_ref, gain_ref, weight_ref, send_ref, xhat_ref, rstd_ref, stage):
    clear_pads(stage)
    for i in range(8):
        put_pair_row(stage, i, res_ref[:, 1 + i])
    merged, xhat, rstd = merge_pairs(stage, gain_ref, weight_ref[...])
    xhat_ref[...] = xhat
    rstd_ref[...] = jnp.broadcast_to(rstd, rstd_ref.shape)
    send_ref[:, 0:1] = res_ref[:, 0:1]
    send_ref[:, 1:5] = fold_merged(merged, 4).astype(BF)


def local_kernel(resA_ref, resB_ref, gain_ref, weight_ref, merged_ref, xhat_ref, rstd_ref, stage):
    clear_pads(stage)
    for i in range(5):
        put_pair_row(stage, i, resA_ref[:, i])
    for i in range(13):
        put_pair_row(stage, 5 + i, resB_ref[:, i])
    merged, xhat, rstd = merge_pairs(stage, gain_ref, weight_ref[...])
    xhat_ref[...] = xhat
    rstd_ref[...] = jnp.broadcast_to(rstd, rstd_ref.shape)
    merged_ref[...] = merged


def local_back_kernel(
    grad_ref, d30_ref, xhat_ref, rstd_ref, gain_ref, weight_ref, dA_ref, dB_ref, stage
):
    merge_pairs_back(
        grad_ref[...], xhat_ref[...], rstd_ref[:, 0:1], gain_ref, weight_ref[...], stage
    )
    for i in range(5):
        dA_ref[:, i] = pair_row(stage, i)
    for i in range(13):
        dB_ref[:, i] = pair_row(stage, 5 + i)
    dB_ref[:, 13] = d30_ref[...]


def receive_kernel(got_ref, xhat_ref, rstd_ref, gain_ref, weight_ref, d_ref, stage):
    grad = unfold_merged(got_ref[:, 1:5].astype(F32))
    merge_pairs_back(grad, xhat_ref[...], rstd_ref[:, 0:1], gain_ref, weight_ref[...], stage)
    d_ref[:, 0:1] = got_ref[:, 0:1]
    for i in range(8):
        d_ref[:, 1 + i] = pair_row(stage, i)


def merge_call(kernel, us, shapes, pairs, *operands):
    return pl.pallas_call(
        kernel,
        out_shape=[jax.ShapeDtypeStruct(shape, kind) for shape, kind in shapes],
        scratch_shapes=[pltpu.VMEM((WT, pairs, 2, 32, 128), F32)],
        compiler_params=params(),
        cost_estimate=cost(us),
    )(*operands)


def middle_kernel(
    merged_ref, resB_ref, next_ref, cot_ref, cta_ref, cha_ref, cdg_ref,
    mg1_ref, mg2_ref, g3_ref, row_ref, col_ref, mw1_hbm, mw2_hbm, p3_hbm, biasA_hbm, biasB_hbm, ow3_hbm,
    dm_ref, d30_ref, dN_ref, so_ref, sta_ref, sha_ref,
    stage, stage2, xhat2, rstd2, cotw, k_s, v_s, qT_s, kT_s, vT_s, probs_s, oT_s, inv_s, doT_s, dqkv_s,
    mw1_ref, mw2_ref, p3_ref, bias_ref, ow3_ref, sems,
):
    fetches = [
        pltpu.make_async_copy(there, here, sems.at[i])
        for i, (there, here) in enumerate(
            (
                (mw1_hbm, mw1_ref),
                (mw2_hbm, mw2_ref),
                (p3_hbm, p3_ref),
                (biasA_hbm, bias_ref.at[:, 0 : ROWS // 2]),
                (biasB_hbm, bias_ref.at[:, ROWS // 2 : ROWS]),
                (ow3_hbm, ow3_ref),
            )
        )
    ]
    for fetch in fetches:
        fetch.start()
    cotw[...] = jnp.zeros((4, 7, 8, 512), F32)
    cotw[0:2, 0:4, 0:7, :] = cot_ref[2:4, 3:7].astype(F32)
    cotw[2:4, 0:4, 0:7, :] = unfold(cta_ref[:, 11:15].astype(F32))
    cotw[0:2, 4:7, 0:7, :] = unfold(cha_ref[:, 3:6].astype(F32))
    cotw[2:4, 4:7, 0:7, :] = unfold(cdg_ref[:, 3:6].astype(F32))

    def put_merged(first, count, values):
        for half in range(2):
            block = values[:, 128 * half : 128 * half + 128].reshape(WT, count, 16, 128)
            for i in range(count):
                stage2[half, :, (first + i) // 2, (first + i) % 2] = block[:, i]

    def take_merged(first, count):
        halves = [
            jnp.concatenate(
                [
                    stage2[half, :, (first + i) // 2, (first + i) % 2].reshape(WT, 1, 16, 128)
                    for i in range(count)
                ],
                1,
            ).reshape(WT * count * 16, 128)
            for half in range(2)
        ]
        return jnp.concatenate(halves, 1)

    put_merged(0, 9, merged_ref[...])
    put_merged(10, 4, unfold_merged(next_ref[:, 1:5].astype(F32)))
    clear_pads(stage)
    put_pair_row(stage, 0, resB_ref[:, 13])
    put_pair_row(stage, 1, next_ref[:, 0])
    fetches[0].wait()
    merged, xhat_seam, rstd_seam = merge_pairs(stage, mg1_ref, mw1_ref[...])
    put_merged(9, 1, merged)
    fetches[1].wait()
    pieces = [
        stage2[half, :, :, q % 2, pl.ds(q // 2, 8, stride=2), :].reshape(ROWS, 128)
        for q in range(4)
        for half in range(2)
    ]
    xhat, rstd = normalise(jnp.concatenate(pieces, 1))
    xhat2[...] = xhat
    rstd2[...] = jnp.broadcast_to(rstd, (ROWS, 128))
    merged_two = dot((xhat * mg2_ref[...]).astype(BF), mw2_ref[...]).astype(BF).astype(F32)
    xhat3, rstd3 = normalise(merged_two)
    n3 = (xhat3 * g3_ref[...]).astype(BF)
    fetches[2].wait()
    packed = [dot(n3, p3_ref[:, 512 * i : 512 * i + 512]) for i in range(3)]
    for g in range(4):
        q, k, v = (part[:, 128 * g : 128 * g + 128] for part in packed)
        q = lengthen((q * (SCALE * LOG2E)).astype(BF))
        k, v = k.astype(BF), v.astype(BF)
        k_s[g] = k
        v_s[g] = v
        qT_s[g] = q.T
        kT_s[g] = lengthen(k).T
        vT_s[g] = lengthen(v).T
    mask = region_mask(col_ref[...], row_ref[...])
    fetches[3].wait()
    fetches[4].wait()

    operands = []
    for g in range(4):

        def keep(h, probs, g=g):
            probs_s[g * 4 + h] = probs

        operands.append((k_s[g], qT_s[g], vT_s[g], mask, lambda h, g=g: bias_ref[g * 4 + h], keep))
    for g, (oT, inverse) in enumerate(attend_four(operands)):
        oT_s[g] = oT
        inv_s[g] = inverse
    fetches[5].wait()
    att = jnp.concatenate([oT_s[g].astype(BF).T[:ROWS] for g in range(4)], 1)
    mixed = dot(att, ow3_ref[...]).astype(BF).astype(F32)
    section = (merged_two + mixed).reshape(4, 7, 8, 512)
    section = fold(section[:, :, 0:7])
    so_ref[...] = section[0:2, 0:4].astype(BF)
    sta_ref[...] = section[2:4].astype(BF)
    sha_ref[...] = section[0:2, 4:7].astype(BF)

    cot = cotw[...].reshape(ROWS, 512)
    cot_long = lengthen(cot.astype(BF))
    doT = dot_nt(ow3_ref[...], cot_long)
    for g in range(4):
        doT_s[g] = doT[128 * g : 128 * g + 128]

    def group_back(g):
        dqkv_s[g], dqkv_s[4 + g], dqkv_s[8 + g] = yield from attend_four_back(
            v_s[g], qT_s[g], kT_s[g], oT_s[g], doT_s[g], inv_s[g], lambda h: probs_s[g * 4 + h]
        )

    stagger(group_back(g) for g in range(4))
    dpacked = jnp.concatenate([dqkv_s[i] for i in range(12)], 1)
    dn3 = dot_nt(dpacked, p3_ref[...])
    dm2 = cot + normalise_back(dn3 * g3_ref[...], xhat3, rstd3)
    dn2 = dot_nt(dm2.astype(BF), mw2_ref[...])
    dg2 = normalise_back(dn2 * mg2_ref[...], xhat2[...], rstd2[:, 0:1])
    for q in range(4):
        for half in range(2):
            at = 256 * q + 128 * half
            stage2[half, :, :, q % 2, pl.ds(q // 2, 8, stride=2), :] = dg2[:, at : at + 128].reshape(
                4, 7, 8, 128
            )

    dm_ref[...] = take_merged(0, 9)
    merge_pairs_back(take_merged(9, 1), xhat_seam, rstd_seam, mg1_ref, mw1_ref[...], stage)
    d30_ref[...] = pair_row(stage, 0)
    dN_ref[:, 0] = pair_row(stage, 1)
    dN_ref[:, 1:5] = fold_merged(take_merged(10, 4), 4).astype(BF)


def middle(*operands):
    shapes = [
        (4, 28, 128), (4, 5, 28, 128), (2, 4, 28, 128), (2, 7, 28, 128), (2, 3, 28, 128),
    ]
    return pl.pallas_call(
        middle_kernel,
        in_specs=[pl.BlockSpec(memory_space=pltpu.VMEM)] * 12
        + [pl.BlockSpec(memory_space=pl.ANY)] * 6,
        out_shape=[jax.ShapeDtypeStruct((576, 256), F32)]
        + [jax.ShapeDtypeStruct(s, BF) for s in shapes],
        scratch_shapes=[
            pltpu.VMEM((4, 1, 2, 32, 128), F32),
            pltpu.VMEM((2, 4, 7, 2, 16, 128), F32),
            pltpu.VMEM((ROWS, 1024), F32),
            pltpu.VMEM((ROWS, 128), F32),
            pltpu.VMEM((4, 7, 8, 512), F32),
            pltpu.VMEM((4, ROWS, 128), BF),
            pltpu.VMEM((4, ROWS, 128), BF),
            pltpu.VMEM((4, 128, LANES), BF),
            pltpu.VMEM((4, 128, LANES), BF),
            pltpu.VMEM((4, 128, LANES), BF),
            pltpu.VMEM((16, ROWS, LANES), BF),
            pltpu.VMEM((4, 128, LANES), F32),
            pltpu.VMEM((4, 8, LANES), F32),
            pltpu.VMEM((4, 128, LANES), F32),
            pltpu.VMEM((12, ROWS, 128), BF),
            pltpu.VMEM((512, 256), BF),
            pltpu.VMEM((1024, 512), BF),
            pltpu.VMEM((512, 1536), BF),
            pltpu.VMEM((HEADS3, ROWS, LANES), F32),
            pltpu.VMEM((512, 512), BF),
            pltpu.SemaphoreType.DMA((6,)),
        ],
        compiler_params=params(28),
        cost_estimate=cost(9),
    )(*operands)


def join_kernel(ta_ref, own_ref, so_ref, grad_ref, section_ref, wide, narrow):
    for t in range(WT):
        wide[:, pl.ds(t, 28, stride=4), :] = (ta_ref if t < 2 else own_ref)[t % 2, 0:11].astype(F32)
        low = (ta_ref[t, 11:15] if t < 2 else so_ref[t - 2]).astype(F32)
        for g in range(4):
            narrow[g, :, pl.ds(t, 7, stride=4), :] = low[:, 7 * g : 7 * g + 7]
    for i in range(11):
        grad_ref[17 + i] = wide[i].reshape(28, 4, 128).astype(BF)
    for i in range(4):
        row = jnp.concatenate([narrow[g, i] for g in range(4)], 1)
        section_ref[3 + i] = row.reshape(7, 4, 512).astype(BF)


JOINED = [
    jax.ShapeDtypeStruct((28, 28, 4, 128), BF),
    jax.ShapeDtypeStruct((7, 7, 4, 512), BF),
]


def join(ta, own, section_own):
    return pl.pallas_call(
        join_kernel,
        out_shape=JOINED,
        scratch_shapes=[pltpu.VMEM((11, 112, 128), F32), pltpu.VMEM((4, 4, 28, 128), F32)],
        compiler_params=params(),
        cost_estimate=cost(2),
    )(ta, own, section_own)


def last_kernel(
    grad_hbm, section_hbm, ta_ref, own_ref, dg_ref, ha_ref, grad_out, section_out,
    wide, narrow, rows, section_rows, sems,
):
    del grad_hbm, section_hbm
    for t in range(WT):
        corner = dg_ref if t < 2 else ha_ref
        wide[0:3, pl.ds(t, 28, stride=4), :] = corner[t % 2, 0:3].astype(F32)
        wide[3:17, pl.ds(t, 28, stride=4), :] = (ta_ref if t < 2 else own_ref)[t % 2].astype(F32)
        high = corner[t % 2, 3:6].astype(F32)
        for g in range(4):
            narrow[g, :, pl.ds(t, 7, stride=4), :] = high[:, 7 * g : 7 * g + 7]
    for i in range(17):
        rows[i] = wide[i].reshape(28, 4, 128).astype(BF)
    copy = pltpu.make_async_copy(rows, grad_out.at[0:17], sems.at[0])
    copy.start()
    for i in range(3):
        row = jnp.concatenate([narrow[g, i] for g in range(4)], 1)
        section_rows[i] = row.reshape(7, 4, 512).astype(BF)
    other = pltpu.make_async_copy(section_rows, section_out.at[0:3], sems.at[1])
    other.start()
    copy.wait()
    other.wait()


def join_last(grad, section, ta, own, dg, ha):
    return pl.pallas_call(
        last_kernel,
        in_specs=[pl.BlockSpec(memory_space=pl.ANY)] * 2
        + [pl.BlockSpec(memory_space=pltpu.VMEM)] * 4,
        out_specs=[pl.BlockSpec(memory_space=pl.ANY)] * 2,
        out_shape=JOINED,
        scratch_shapes=[
            pltpu.VMEM((17, 112, 128), F32),
            pltpu.VMEM((4, 3, 28, 128), F32),
            pltpu.VMEM((17, 28, 4, 128), BF),
            pltpu.VMEM((3, 7, 4, 512), BF),
            pltpu.SemaphoreType.DMA((2,)),
        ],
        input_output_aliases={0: 0, 1: 1},
        compiler_params=params(),
        cost_estimate=cost(1),
    )(grad, section, ta, own, dg, ha)


IN_ORDER = Layout(major_to_minor=(0, 1, 2, 3))


def inward(values):
    return with_layout_constraint(jnp.transpose(values, (1, 2, 0, 3)), IN_ORDER)


def outward(values):
    return jnp.transpose(with_layout_constraint(values, IN_ORDER), (2, 0, 1, 3))


def send(values, axes, by):
    axes = axes.split()
    sizes = [lax.axis_size(a) for a in axes]
    if len(axes) == 1:
        pairs = [(i, (i + by) % sizes[0]) for i in range(sizes[0])]
    else:
        n, m = sizes
        pairs = [
            (i * m + j, (i + by) % n * m + (j + by) % m) for i in range(n) for j in range(m)
        ]
    return lax.ppermute(values, tuple(axes), pairs)


def per_device(
    tokens,
    regions_one,
    regions_three,
    gain_one,
    projection_one,
    outward_one,
    table_one,
    merge_gain_one,
    merge_weight_one,
    merge_gain_two,
    merge_weight_two,
    gain_three,
    projection_three,
    outward_three,
    table_three,
    cotangent,
):
    (early,) = arrange(early_kernel, (14,), tokens)
    ta_early = send(inward(early), "ta", -1)
    late, ha_late, dg_late = arrange(late_kernel, (15, 6, 6), tokens, cotangent)
    ha_late = send(ha_late, "ha", -1)
    dg_late = send(dg_late, "ha ta", -1)
    ta_late = send(inward(late), "ta", -1)
    bias_one, spread, row_one, row_three, col_one, col_three = prepare(
        table_one, table_three, regions_one, regions_three
    )
    gain, merge_gain, seam = gain_one[None], merge_gain_one[None], merge_weight_one
    args = (gain, projection_one, outward_one, bias_one, spread)
    (res_send, res_a, bias_a), saved_a = front(False, (tokens, outward(ta_early)), *args, row_one, col_one)
    row_send, *early_norm = merge_call(
        send_kernel, 0.5, [((4, 5, 28, 128), BF), ((256, 512), F32), ((256, 128), F32)], 4,
        res_send, merge_gain, seam,
    )
    row_next = send(row_send, "ha", -1)
    ta_late, res_a = lax.optimization_barrier((ta_late, res_a))
    ta_late = outward(ta_late)
    (res_b, bias_b), saved_b = front(True, (tokens, ta_late, ha_late, dg_late), *args, row_one, col_one)
    merged, *local_norm = merge_call(
        local_kernel, 0.1, [((576, 256), F32), ((576, 512), F32), ((576, 128), F32)], 9,
        res_a, res_b, merge_gain, seam,
    )
    row_next, merged = lax.optimization_barrier((row_next, merged))
    d_merged, d_30, d_send, sec_own, sec_ta, sec_ha = middle(
        merged, res_b, row_next, cotangent, ta_late, ha_late, dg_late,
        merge_gain, merge_gain_two[None], gain_three[None], row_three, col_three,
        merge_weight_one, merge_weight_two, projection_three, bias_a, bias_b, outward_three,
    )
    d_prev = send(d_send, "ha", 1)
    d_a, d_b = merge_call(
        local_back_kernel, 1, [((4, 5, 28, 128), BF), ((4, 14, 28, 128), BF)], 9,
        d_merged, d_30, *local_norm, merge_gain, seam,
    )
    own_b, ta_b, ha_b = back(
        True, (d_b, sec_ta, sec_ha), gain, projection_one, outward_one, saved_b
    )
    d_prev, own_b = lax.optimization_barrier((d_prev, own_b))
    ta_b = send(inward(ta_b), "ta", 1)
    ha_b = send(ha_b, "ha", 1)
    (d_first,) = merge_call(
        receive_kernel, 0.5, [((4, 9, 28, 128), BF)], 4, d_prev, *early_norm, merge_gain, seam
    )
    own_a, ta_a = back(False, (d_first, d_a), gain, projection_one, outward_one, saved_a)
    ta_b, ha_b, own_a = lax.optimization_barrier((ta_b, ha_b, own_a))
    ta_a = send(inward(ta_a), "ta", 1)
    dg_b = send(ha_b[2:], "ta", 1)
    grad, section = join(outward(ta_b), own_b, sec_own)
    ta_a, dg_b, grad = lax.optimization_barrier((ta_a, dg_b, grad))
    grad, section = join_last(grad, section, outward(ta_a), own_a, dg_b, ha_b)
    return (jnp.transpose(section, (2, 0, 1, 3)), jnp.transpose(grad, (2, 0, 1, 3)))


def solution(mesh):
    tile = P(("col", "ta"), "ha", None, None)
    ids = P(("col", "ta"), "ha", None)
    in_specs = (tile, ids, ids) + (P(),) * 12 + (tile,)
    return jax.shard_map(
        per_device, mesh=mesh, in_specs=in_specs, out_specs=(tile, tile), check_vma=False
    )
```

profile of v0, /device:TPU:0, one launch (start us, length us, event | category | flops | bytes accessed | tf_op | source)
XLA Modules:
  0.0 56.3 jit_solution(6957587013498676435)
XLA Ops:
  0.6 1.3 %copy.38.tok_ref.refs_0_ = bf16[4,28,28,128]{3,2,1,0:T(8,128)(2,1)S(1)} copy(bf16[4,28,28,128]{3,0,2,1:T(4,128)(2,1)} %param.17) | data formatting | bytes 1605632 | tf_op args[0]
  2.1 0.2 copy.64
  2.3 3.0 %collective-permute-start = (bf16[14,28,2,128]{3,2,1,0:T(2,128)(2,1)S(1)}, bf16[14,28,2,128]{3,2,1,0:T(2,128)(2,1)S(1)}, u32[]{:S(2)}, u32[]{:S(2)}) collective-permute-start(bf16[14,28,2,128]{3,2,1,0:T(2,128)(2,1)S(1)} %bitcast.57), channel_id=1, source_target_pairs={{0,2},{2,0},{1,3},{3,1},{4,6},{6,4},{5,7},{7,5},{8,10},{10,8},{9,1... | collective-permute-start | bytes 602120 | tf_op jit(solution)/shard_map/ppermute | solution.py:895
  5.7 5.1 %collective-permute-start.3 = (bf16[2,6,28,128]{3,2,1,0:T(8,128)(2,1)S(1)}, bf16[2,6,28,128]{3,2,1,0:T(8,128)(2,1)S(1)}, u32[]{:S(2)}, u32[]{:S(2)}) collective-permute-start(bf16[2,6,28,128]{3,2,1,0:T(8,128)(2,1)S(1)} %get-tuple-element.73), channel_id=1, source_target_pairs={{0,28},{4,0},{8,4},{12,8},{16,12},{20,16},{24,20},{28,24},{1,29},{... | collective-permute-start | bytes 258056 | tf_op jit(solution)/shard_map/ppermute | solution.py:895
  10.7 1.4 %collective-permute-start.4 = (bf16[2,6,28,128]{3,2,1,0:T(8,128)(2,1)S(1)}, bf16[2,6,28,128]{3,2,1,0:T(8,128)(2,1)S(1)}, u32[]{:S(2)}, u32[]{:S(2)}) collective-permute-start(bf16[2,6,28,128]{3,2,1,0:T(8,128)(2,1)S(1)} %get-tuple-element.74), channel_id=1, source_target_pairs={{0,30},{2,28},{4,2},{6,0},{8,6},{10,4},{12,10},{14,8},{16,14},{18,... | collective-permute-start | bytes 258056 | tf_op jit(solution)/shard_map/ppermute | solution.py:895
  12.3 1.7 %shard_map.177 = (f32[4,224,256]{2,1,0:T(8,128)S(1)}, f32[7,192,128]{2,1,0:T(8,128)S(1)}, f32[16,1,256]{2,1,0:T(1,128)S(1)}, f32[1,256]{1,0:T(1,128)S(1)}, f32[1...) custom-call(f32[4,1183]{1,0:T(4,128)S(1)} %bitcast.48, f32[16,1183]{1,0:T(8,128)S(1)} %bitcast.46, ...), custom_call_target="tpu_custom_call" | custom-call | flops 1650000000 | bytes 1500000 | tf_op jit(solution)/shard_map/pallas_call | solution.py:267
  14.0 3.9 %shard_map.178 = (bf16[4,9,28,128]{3,2,1,0:T(8,128)(2,1)S(1)}, bf16[4,5,28,128]{3,2,1,0:T(8,128)(2,1)S(1)}, f32[16,112,256]{2,1,0:T(8,128)S(1)}, bf16[8,224,128]...) custom-call(bf16[4,28,28,128]{3,2,1,0:T(8,128)(2,1)S(1)} %copy.38.to, ...), custom_call_target="tpu_custom_call" | custom-call | flops 5059999744 | bytes 4600000 | tf_op jit(solution)/shard_map/pallas_call | solution.py:437
  17.9 0.4 shard_map.179
  18.4 2.5 %collective-permute-start.1 = (bf16[4,5,28,128]{3,2,1,0:T(8,128)(2,1)S(1)}, bf16[4,5,28,128]{3,2,1,0:T(8,128)(2,1)S(1)}, u32[]{:S(2)}, u32[]{:S(2)}) collective-permute-start(bf16[4,5,28,128]{3,2,1,0:T(8,128)(2,1)S(1)} %get-tuple-element.68), channel_id=1, source_target_pairs={{0,28},{4,0},{8,4},{12,8},{16,12},{20,16},{24,20},{28,24},{1,29},{... | collective-permute-start | bytes 430088 | tf_op jit(solution)/shard_map/ppermute | solution.py:895
  21.0 3.9 %shard_map.181 = (bf16[4,14,28,128]{3,2,1,0:T(8,128)(2,1)S(1)}, f32[16,112,256]{2,1,0:T(8,128)S(1)}, bf16[8,224,128]{2,1,0:T(8,128)(2,1)S(1)}, bf16[8,224,256]{2...) custom-call(bf16[4,28,28,128]{3,2,1,0:T(8,128)(2,1)S(1)} %copy.38.to, ...), custom_call_target="tpu_custom_call" | custom-call | flops 5059999744 | bytes 4600000 | tf_op jit(solution)/shard_map/pallas_call | solution.py:437
  24.9 0.6 %shard_map.182 = (f32[576,256]{1,0:T(8,128)S(1)}, f32[576,512]{1,0:T(8,128)S(1)}, f32[576,128]{1,0:T(8,128)S(1)}) custom-call(bf16[4,5,28,128]{3,2,1,0:T(8,128)(2,1)S(1)} %get-tuple-element.71.resA_ref, bf16[4,14,28,128]{3,2,1,0:T(8,128)(2,1)S(1)} %get-tuple-element.75.resB_ref, f32[1,512]{1,0:T(1,128)S(1)} %bitcast.42, bf16[512,256]{1,0:T(8,128)(2,1)S(1)} %copy-done), custom_call_target="tpu_custom_call" | custom-call | flops 110000000 | bytes 100000 | tf_op jit(solution)/shard_map/pallas_call | solution.py:621
  25.6 7.7 %shard_map.183 = (f32[576,256]{1,0:T(8,128)S(1)}, bf16[4,28,128]{2,1,0:T(8,128)(2,1)S(1)}, bf16[4,5,28,128]{3,2,1,0:T(8,128)(2,1)S(1)}, bf16[2,4,28,128]{3,2,1,0...) custom-call(f32[576,256]{1,0:T(8,128)S(1)} %get-tuple-element.77.merged_ref, ...), custom_call_target="tpu_custom_call" | custom-call | flops 9900000256 | bytes 9000000 | tf_op jit(solution)/shard_map/pallas_call | solution.py:766
  33.3 1.1 %collective-permute-start.5 = (bf16[4,5,28,128]{3,2,1,0:T(8,128)(2,1)S(1)}, bf16[4,5,28,128]{3,2,1,0:T(8,128)(2,1)S(1)}, u32[]{:S(2)}, u32[]{:S(2)}) collective-permute-start(bf16[4,5,28,128]{3,2,1,0:T(8,128)(2,1)S(1)} %get-tuple-element.83), channel_id=1, source_target_pairs={{0,4},{4,8},{8,12},{12,16},{16,20},{20,24},{24,28},{28,0},{1,5},{5... | collective-permute-start | bytes 430088 | tf_op jit(solution)/shard_map/ppermute | solution.py:895
  34.3 0.7 %shard_map.184 = (bf16[4,5,28,128]{3,2,1,0:T(8,128)(2,1)S(1)}, bf16[4,14,28,128]{3,2,1,0:T(8,128)(2,1)S(1)}) custom-call(f32[576,256]{1,0:T(8,128)S(1)} %get-tuple-element.84.grad_ref, bf16[4,28,128]{2,1,0:T(8,128)(2,1)S(1)} %get-tuple-element.85.d30_ref, f32[576,512]{1,0:T(8,128)S(1)} %get-tuple-element.86.xhat_ref, ...), custom_call_target="tpu_custom_call" | custom-call | flops 1100000000 | bytes 1000000 | tf_op jit(solution)/shard_map/pallas_call | solution.py:621
  35.0 5.1 %shard_map.185 = (bf16[2,11,28,128]{3,2,1,0:T(8,128)(2,1)S(1)}, bf16[2,15,28,128]{3,2,1,0:T(8,128)(2,1)S(1)}, bf16[4,6,28,128]{3,2,1,0:T(8,128)(2,1)S(1)}) custom-call(bf16[4,14,28,128]{3,2,1,0:T(8,128)(2,1)S(1)} %get-tuple-element.88.refs_0_, bf16[2,7,28,128]{3,2,1,0:T(8,128)(2,1)S(1)} %get-tuple-element.89.refs_1_, ...), custom_call_target="tpu_custom_call" | custom-call | flops 6049999872 | bytes 5500000 | tf_op jit(solution)/shard_map/pallas_call | solution.py:515
  40.4 0.8 %collective-permute-start.7 = (bf16[15,28,2,128]{3,2,1,0:T(2,128)(2,1)S(1)}, bf16[15,28,2,128]{3,2,1,0:T(2,128)(2,1)S(1)}, u32[]{:S(2)}, u32[]{:S(2)}) collective-permute-start(bf16[15,28,2,128]{3,2,1,0:T(2,128)(2,1)S(1)} %bitcast.56), channel_id=1, source_target_pairs={{0,2},{2,0},{1,3},{3,1},{4,6},{6,4},{5,7},{7,5},{8,10},{10,8},{9,1... | collective-permute-start | bytes 645128 | tf_op jit(solution)/shard_map/ppermute | solution.py:895
  41.2 1.2 %collective-permute-start.8 = (bf16[4,6,28,128]{3,2,1,0:T(8,128)(2,1)S(1)}, bf16[4,6,28,128]{3,2,1,0:T(8,128)(2,1)S(1)}, u32[]{:S(2)}, u32[]{:S(2)}) collective-permute-start(bf16[4,6,28,128]{3,2,1,0:T(8,128)(2,1)S(1)} %get-tuple-element.110), channel_id=1, source_target_pairs={{0,4},{4,8},{8,12},{12,16},{16,20},{20,24},{24,28},{28,0},{1,5},{5... | collective-permute-start | bytes 516104 | tf_op jit(solution)/shard_map/ppermute | solution.py:895
  42.4 0.4 shard_map.186.refs_0_
  42.8 5.1 %shard_map.187 = (bf16[2,14,28,128]{3,2,1,0:T(8,128)(2,1)S(1)}, bf16[2,14,28,128]{3,2,1,0:T(8,128)(2,1)S(1)}) custom-call(bf16[4,9,28,128]{3,2,1,0:T(8,128)(2,1)S(1)} %shard_map.186.refs_0_, bf16[4,5,28,128]{3,2,1,0:T(8,128)(2,1)S(1)} %get-tuple-element.101.refs_1_, f32[1,128]{1,0:T(1,128)S(1)} %bitcast.54, bf16[128,384]{1,0:T(8,128)(2,1)S(1)} %copy-done.5, ...), custom_call_target="tpu_custom_call" | custom-call | flops 6049999872 | bytes 5500000 | tf_op jit(solution)/shard_map/pallas_call | solution.py:515
  48.2 1.5 %collective-permute-start.6 = (bf16[14,28,2,128]{3,2,1,0:T(2,128)(2,1)S(1)}, bf16[14,28,2,128]{3,2,1,0:T(2,128)(2,1)S(1)}, u32[]{:S(2)}, u32[]{:S(2)}) collective-permute-start(bf16[14,28,2,128]{3,2,1,0:T(2,128)(2,1)S(1)} %bitcast.58), channel_id=1, source_target_pairs={{0,2},{2,0},{1,3},{3,1},{4,6},{6,4},{5,7},{7,5},{8,10},{10,8},{9,1... | collective-permute-start | bytes 602120 | tf_op jit(solution)/shard_map/ppermute | solution.py:895
  49.7 1.2 %collective-permute-start.9 = (bf16[2,6,28,128]{3,2,1,0:T(8,128)(2,1)S(1)}, bf16[2,6,28,128]{3,2,1,0:T(8,128)(2,1)S(1)}, u32[]{:S(2)}, u32[]{:S(2)}) collective-permute-start(bf16[2,6,28,128]{3,2,1,0:T(8,128)(2,1)S(1)} %slice.3), channel_id=1, source_target_pairs={{0,2},{2,0},{1,3},{3,1},{4,6},{6,4},{5,7},{7,5},{8,10},{10,8},{9,1... | collective-permute-start | bytes 258056 | tf_op jit(solution)/shard_map/ppermute | solution.py:895
  50.9 1.2 %shard_map.188 = (bf16[28,28,4,128]{3,2,1,0:T(4,128)(2,1)}, bf16[7,7,4,512]{3,2,1,0:T(4,128)(2,1)}) custom-call(bf16[2,15,28,128]{3,2,1,0:T(8,128)(2,1)S(1)} %bitcast.38, bf16[2,11,28,128]{3,2,1,0:T(8,128)(2,1)S(1)} %get-tuple-element.114.own_ref, bf16[2,4,28,128]{3,2,1,0:T(8,128)(2,1)S(1)} %get-tuple-element.115.so_ref), custom_call_target="tpu_custom_call" | custom-call | flops 2200000000 | bytes 2000000 | tf_op jit(solution)/shard_map/pallas_call | solution.py:820
  52.1 2.9 %collective-permute-done.9.dg_ref = bf16[2,6,28,128]{3,2,1,0:T(8,128)(2,1)S(1)} collective-permute-done((bf16[2,6,28,128]{3,2,1,0:T(8,128)(2,1)S(1)}, bf16[2,6,28,128]{3,2,1,0:T(8,128)(2,1)S(1)}, u32[]{:S(2)}, u32[]{:S(2)}) %collective-permute-start.9) | collective-permute-done | bytes 86048 | tf_op jit(solution)/shard_map/ppermute | solution.py:895
  55.0 1.1 %shard_map.189 = (bf16[28,28,4,128]{3,2,1,0:T(4,128)(2,1)}, bf16[7,7,4,512]{3,2,1,0:T(4,128)(2,1)}) custom-call(bf16[28,28,4,128]{3,2,1,0:T(4,128)(2,1)} %get-tuple-element.117.grad_hbm, bf16[7,7,4,512]{3,2,1,0:T(4,128)(2,1)} %get-tuple-element.118.section_hbm, bf16[2,14,28,128]{3,2,1,0:T(8,128)(2,1)S(1)} %bitcast.40, ...), custom_call_target="tpu_custom_call", output_to_operand_aliasing={{0}: (0, {}), {1}: (1, {})} | custom-call | flops 1100000000 | bytes 1000000 | tf_op jit(solution)/shard_map/pallas_call | solution.py:855
  (54 shorter events, 1.0 us)
Async XLA Ops:
  0.6 4.7 %copy-start.14 = (bf16[4,7,7,512]{3,0,2,1:T(4,128)(2,1)S(1)}, bf16[4,7,7,512]{3,0,2,1:T(4,128)(2,1)}, u32[]{:S(2)}) copy-start(bf16[4,7,7,512]{3,0,2,1:T(4,128)(2,1)} %param.32) | copy-start | bytes 602116
  2.0 10.2 %copy-start.15 = (s32[4,7,7]{2,0,1:T(4,128)S(1)}, s32[4,7,7]{2,0,1:T(4,128)}, u32[]{:S(2)}) copy-start(s32[4,7,7]{2,0,1:T(4,128)} %param.19) | copy-start | bytes 2356
  2.0 10.2 %copy-start.6 = (f32[1183,16]{0,1:T(8,128)S(1)}, f32[1183,16]{0,1:T(8,128)}, u32[]{:S(2)}) copy-start(f32[1183,16]{0,1:T(8,128)} %param.31) | copy-start | bytes 227140
  2.0 10.2 %copy-start.7 = (s32[4,28,28]{2,0,1:T(4,128)S(1)}, s32[4,28,28]{2,0,1:T(4,128)}, u32[]{:S(2)}) copy-start(s32[4,28,28]{2,0,1:T(4,128)} %param.18) | copy-start | bytes 37636
  2.0 10.2 %copy-start.9 = (f32[1183,4]{0,1:T(4,128)S(1)}, f32[1183,4]{0,1:T(4,128)}, u32[]{:S(2)}) copy-start(f32[1183,4]{0,1:T(4,128)} %param.23) | copy-start | bytes 56788
  2.0 10.2 %copy-start.13 = (bf16[256,1024]{1,0:T(8,128)(2,1)S(1)}, bf16[256,1024]{1,0:T(8,128)(2,1)}, u32[]{:S(2)}) copy-start(bf16[256,1024]{1,0:T(8,128)(2,1)} %constant.2.clone.s_ref) | copy-start | bytes 1572868
  2.3 11.7 %collective-permute-start = (bf16[14,28,2,128]{3,2,1,0:T(2,128)(2,1)S(1)}, bf16[14,28,2,128]{3,2,1,0:T(2,128)(2,1)S(1)}, u32[]{:S(2)}, u32[]{:S(2)}) collective-permute-start(bf16[14,28,2,128]{3,2,1,0:T(2,128)(2,1)S(1)} %bitcast.57), channel_id=1, source_target_pairs={{0,2},{2,0},{1,3},{3,1},{4,6},{6,4},{5,7},{7,5},{8,10},{10,8},{9,1... | collective-permute-start | bytes 602120 | tf_op jit(solution)/shard_map/ppermute | solution.py:895
  5.6 15.3 %collective-permute-start.2 = (bf16[15,28,2,128]{3,2,1,0:T(2,128)(2,1)S(1)}, bf16[15,28,2,128]{3,2,1,0:T(2,128)(2,1)S(1)}, u32[]{:S(2)}, u32[]{:S(2)}) collective-permute-start(bf16[15,28,2,128]{3,2,1,0:T(2,128)(2,1)S(1)} %bitcast.55), channel_id=1, source_target_pairs={{0,2},{2,0},{1,3},{3,1},{4,6},{6,4},{5,7},{7,5},{8,10},{10,8},{9,1... | collective-permute-start | bytes 645128 | tf_op jit(solution)/shard_map/ppermute | solution.py:895
  5.7 15.3 %collective-permute-start.3 = (bf16[2,6,28,128]{3,2,1,0:T(8,128)(2,1)S(1)}, bf16[2,6,28,128]{3,2,1,0:T(8,128)(2,1)S(1)}, u32[]{:S(2)}, u32[]{:S(2)}) collective-permute-start(bf16[2,6,28,128]{3,2,1,0:T(8,128)(2,1)S(1)} %get-tuple-element.73), channel_id=1, source_target_pairs={{0,28},{4,0},{8,4},{12,8},{16,12},{20,16},{24,20},{28,24},{1,29},{... | collective-permute-start | bytes 258056 | tf_op jit(solution)/shard_map/ppermute | solution.py:895
  10.7 10.2 %collective-permute-start.4 = (bf16[2,6,28,128]{3,2,1,0:T(8,128)(2,1)S(1)}, bf16[2,6,28,128]{3,2,1,0:T(8,128)(2,1)S(1)}, u32[]{:S(2)}, u32[]{:S(2)}) collective-permute-start(bf16[2,6,28,128]{3,2,1,0:T(8,128)(2,1)S(1)} %get-tuple-element.74), channel_id=1, source_target_pairs={{0,30},{2,28},{4,2},{6,0},{8,6},{10,4},{12,10},{14,8},{16,14},{18,... | collective-permute-start | bytes 258056 | tf_op jit(solution)/shard_map/ppermute | solution.py:895
  12.2 1.8 %copy-start.5 = (bf16[128,384]{1,0:T(8,128)(2,1)S(1)}, bf16[128,384]{1,0:T(8,128)(2,1)}, u32[]{:S(2)}) copy-start(bf16[128,384]{1,0:T(8,128)(2,1)} %refs_3_.3) | copy-start | bytes 294916
  14.0 3.9 %copy-start = (bf16[512,256]{1,0:T(8,128)(2,1)S(1)}, bf16[512,256]{1,0:T(8,128)(2,1)}, u32[]{:S(2)}) copy-start(bf16[512,256]{1,0:T(8,128)(2,1)} %weight_ref.7) | copy-start | bytes 786436
  14.0 3.9 %copy-start.1 = (f32[512]{0:T(512)S(1)}, f32[512]{0:T(512)}, u32[]{:S(2)}) copy-start(f32[512]{0:T(512)} %param.24) | copy-start | bytes 6148
  18.4 7.1 %collective-permute-start.1 = (bf16[4,5,28,128]{3,2,1,0:T(8,128)(2,1)S(1)}, bf16[4,5,28,128]{3,2,1,0:T(8,128)(2,1)S(1)}, u32[]{:S(2)}, u32[]{:S(2)}) collective-permute-start(bf16[4,5,28,128]{3,2,1,0:T(8,128)(2,1)S(1)} %get-tuple-element.68), channel_id=1, source_target_pairs={{0,28},{4,0},{8,4},{12,8},{16,12},{20,16},{24,20},{28,24},{1,29},{... | collective-permute-start | bytes 430088 | tf_op jit(solution)/shard_map/ppermute | solution.py:895
  20.9 4.6 %copy-start.2 = (bf16[512,1536]{1,0:T(8,128)(2,1)S(1)}, bf16[512,1536]{1,0:T(8,128)(2,1)}, u32[]{:S(2)}) copy-start(bf16[512,1536]{1,0:T(8,128)(2,1)} %p3_hbm.1) | copy-start | bytes 4718596
  21.0 4.6 %copy-start.3 = (bf16[1024,512]{1,0:T(8,128)(2,1)S(1)}, bf16[1024,512]{1,0:T(8,128)(2,1)}, u32[]{:S(2)}) copy-start(bf16[1024,512]{1,0:T(8,128)(2,1)} %mw2_hbm.1) | copy-start | bytes 3145732
  21.0 4.6 %copy-start.4 = (bf16[512,512]{1,0:T(8,128)(2,1)S(1)}, bf16[512,512]{1,0:T(8,128)(2,1)}, u32[]{:S(2)}) copy-start(bf16[512,512]{1,0:T(8,128)(2,1)} %ow3_hbm.1) | copy-start | bytes 1572868
  21.0 4.6 %copy-start.10 = (f32[1024]{0:T(1024)S(1)}, f32[1024]{0:T(1024)}, u32[]{:S(2)}) copy-start(f32[1024]{0:T(1024)} %param.26) | copy-start | bytes 12292
  21.0 4.6 %copy-start.11 = (f32[512]{0:T(512)S(1)}, f32[512]{0:T(512)}, u32[]{:S(2)}) copy-start(f32[512]{0:T(512)} %param.28) | copy-start | bytes 6148
  33.3 9.1 %collective-permute-start.5 = (bf16[4,5,28,128]{3,2,1,0:T(8,128)(2,1)S(1)}, bf16[4,5,28,128]{3,2,1,0:T(8,128)(2,1)S(1)}, u32[]{:S(2)}, u32[]{:S(2)}) collective-permute-start(bf16[4,5,28,128]{3,2,1,0:T(8,128)(2,1)S(1)} %get-tuple-element.83), channel_id=1, source_target_pairs={{0,4},{4,8},{8,12},{12,16},{16,20},{20,24},{24,28},{28,0},{1,5},{5... | collective-permute-start | bytes 430088 | tf_op jit(solution)/shard_map/ppermute | solution.py:895
  40.4 9.3 %collective-permute-start.7 = (bf16[15,28,2,128]{3,2,1,0:T(2,128)(2,1)S(1)}, bf16[15,28,2,128]{3,2,1,0:T(2,128)(2,1)S(1)}, u32[]{:S(2)}, u32[]{:S(2)}) collective-permute-start(bf16[15,28,2,128]{3,2,1,0:T(2,128)(2,1)S(1)} %bitcast.56), channel_id=1, source_target_pairs={{0,2},{2,0},{1,3},{3,1},{4,6},{6,4},{5,7},{7,5},{8,10},{10,8},{9,1... | collective-permute-start | bytes 645128 | tf_op jit(solution)/shard_map/ppermute | solution.py:895
  41.2 8.5 %collective-permute-start.8 = (bf16[4,6,28,128]{3,2,1,0:T(8,128)(2,1)S(1)}, bf16[4,6,28,128]{3,2,1,0:T(8,128)(2,1)S(1)}, u32[]{:S(2)}, u32[]{:S(2)}) collective-permute-start(bf16[4,6,28,128]{3,2,1,0:T(8,128)(2,1)S(1)} %get-tuple-element.110), channel_id=1, source_target_pairs={{0,4},{4,8},{8,12},{12,16},{16,20},{20,24},{24,28},{28,0},{1,5},{5... | collective-permute-start | bytes 516104 | tf_op jit(solution)/shard_map/ppermute | solution.py:895
  48.2 6.8 %collective-permute-start.6 = (bf16[14,28,2,128]{3,2,1,0:T(2,128)(2,1)S(1)}, bf16[14,28,2,128]{3,2,1,0:T(2,128)(2,1)S(1)}, u32[]{:S(2)}, u32[]{:S(2)}) collective-permute-start(bf16[14,28,2,128]{3,2,1,0:T(2,128)(2,1)S(1)} %bitcast.58), channel_id=1, source_target_pairs={{0,2},{2,0},{1,3},{3,1},{4,6},{6,4},{5,7},{7,5},{8,10},{10,8},{9,1... | collective-permute-start | bytes 602120 | tf_op jit(solution)/shard_map/ppermute | solution.py:895
  49.7 5.3 %collective-permute-start.9 = (bf16[2,6,28,128]{3,2,1,0:T(8,128)(2,1)S(1)}, bf16[2,6,28,128]{3,2,1,0:T(8,128)(2,1)S(1)}, u32[]{:S(2)}, u32[]{:S(2)}) collective-permute-start(bf16[2,6,28,128]{3,2,1,0:T(8,128)(2,1)S(1)} %slice.3), channel_id=1, source_target_pairs={{0,2},{2,0},{1,3},{3,1},{4,6},{6,4},{5,7},{7,5},{8,10},{10,8},{9,1... | collective-permute-start | bytes 258056 | tf_op jit(solution)/shard_map/ppermute | solution.py:895
  (2 other events, 3.5 us)
where the time goes:
time: 56.5 us; the launch traced here: 56.3 us
  Pallas kernels  31.9 us (56%)
  starting transfers between devices  17.9 us (32%)
  waiting for transfers between devices  2.93 us (5%)
  local copies, waits for them, and re-layouts  2.36 us (4%)
  between operations  1.25 us (2%)
    ppermute x10, starting transfers between devices, send(): return lax.ppermute(values, tuple(axes), pairs)  17.9 us
    pallas_call x2, Pallas kernels, back(): pl.pallas_call(functools.partial(back_kernel, late), out_shape=[jax.Shape...  10.3 us
    pallas_call x2, Pallas kernels, front(): pl.pallas_call(functools.partial(front_kernel, late), out_shape=[jax.Shap...  7.72 us
    pallas_call x1, Pallas kernels, middle(): pl.pallas_call(middle_kernel, in_specs=[pl.BlockSpec(memory_space=pltpu.V...  7.66 us
    ppermute x10, waiting for transfers between devices, send(): return lax.ppermute(values, tuple(axes), pairs)  2.93 us
    pallas_call x4, Pallas kernels, merge_call(): pl.pallas_call(kernel, out_shape=[jax.ShapeDtypeStruct(shape, kind) for s...  2.21 us
    pallas_call x1, Pallas kernels, prepare(): pl.pallas_call(prepare_kernel, out_shape=(jax.ShapeDtypeStruct((HEADS1, R...  1.68 us
    unnamed x34, local copies, waits for them, and re-layouts  1.46 us
  transfers between devices with their start and end apart: 10, of which 1 were waited for; matrix products, arithmetic and copies ran while one was open for 1% of the time, Pallas kernels for 41%

commit v1 on v0

--- a/solution.py
+++ b/solution.py
@@ -629,26 +629,10 @@
 
 def middle_kernel(
     merged_ref, resB_ref, next_ref, cot_ref, cta_ref, cha_ref, cdg_ref,
-    mg1_ref, mg2_ref, g3_ref, row_ref, col_ref, mw1_hbm, mw2_hbm, p3_hbm, biasA_hbm, biasB_hbm, ow3_hbm,
+    mg1_ref, mg2_ref, g3_ref, row_ref, col_ref, mw1_ref, mw2_ref, p3_ref, biasA_ref, biasB_ref, ow3_ref,
     dm_ref, d30_ref, dN_ref, so_ref, sta_ref, sha_ref,
     stage, stage2, xhat2, rstd2, cotw, k_s, v_s, qT_s, kT_s, vT_s, probs_s, oT_s, inv_s, doT_s, dqkv_s,
-    mw1_ref, mw2_ref, p3_ref, bias_ref, ow3_ref, sems,
 ):
-    fetches = [
-        pltpu.make_async_copy(there, here, sems.at[i])
-        for i, (there, here) in enumerate(
-            (
-                (mw1_hbm, mw1_ref),
-                (mw2_hbm, mw2_ref),
-                (p3_hbm, p3_ref),
-                (biasA_hbm, bias_ref.at[:, 0 : ROWS // 2]),
-                (biasB_hbm, bias_ref.at[:, ROWS // 2 : ROWS]),
-                (ow3_hbm, ow3_ref),
-            )
-        )
-    ]
-    for fetch in fetches:
-        fetch.start()
     cotw[...] = jnp.zeros((4, 7, 8, 512), F32)
     cotw[0:2, 0:4, 0:7, :] = cot_ref[2:4, 3:7].astype(F32)
     cotw[2:4, 0:4, 0:7, :] = unfold(cta_ref[:, 11:15].astype(F32))
@@ -679,10 +663,8 @@
     clear_pads(stage)
     put_pair_row(stage, 0, resB_ref[:, 13])
     put_pair_row(stage, 1, next_ref[:, 0])
-    fetches[0].wait()
     merged, xhat_seam, rstd_seam = merge_pairs(stage, mg1_ref, mw1_ref[...])
     put_merged(9, 1, merged)
-    fetches[1].wait()
     pieces = [
         stage2[half, :, :, q % 2, pl.ds(q // 2, 8, stride=2), :].reshape(ROWS, 128)
         for q in range(4)
@@ -694,7 +676,6 @@
     merged_two = dot((xhat * mg2_ref[...]).astype(BF), mw2_ref[...]).astype(BF).astype(F32)
     xhat3, rstd3 = normalise(merged_two)
     n3 = (xhat3 * g3_ref[...]).astype(BF)
-    fetches[2].wait()
     packed = [dot(n3, p3_ref[:, 512 * i : 512 * i + 512]) for i in range(3)]
     for g in range(4):
         q, k, v = (part[:, 128 * g : 128 * g + 128] for part in packed)
@@ -705,9 +686,11 @@
         qT_s[g] = q.T
         kT_s[g] = lengthen(k).T
         vT_s[g] = lengthen(v).T
+
+    def bias_at(head):
+        return jnp.concatenate([biasA_ref[head], biasB_ref[head]], 0)
+
     mask = region_mask(col_ref[...], row_ref[...])
-    fetches[3].wait()
-    fetches[4].wait()
 
     operands = []
     for g in range(4):
@@ -715,11 +698,10 @@
         def keep(h, probs, g=g):
             probs_s[g * 4 + h] = probs
 
-        operands.append((k_s[g], qT_s[g], vT_s[g], mask, lambda h, g=g: bias_ref[g * 4 + h], keep))
+        operands.append((k_s[g], qT_s[g], vT_s[g], mask, lambda h, g=g: bias_at(g * 4 + h), keep))
     for g, (oT, inverse) in enumerate(attend_four(operands)):
         oT_s[g] = oT
         inv_s[g] = inverse
-    fetches[5].wait()
     att = jnp.concatenate([oT_s[g].astype(BF).T[:ROWS] for g in range(4)], 1)
     mixed = dot(att, ow3_ref[...]).astype(BF).astype(F32)
     section = (merged_two + mixed).reshape(4, 7, 8, 512)
@@ -765,8 +747,6 @@
     ]
     return pl.pallas_call(
         middle_kernel,
-        in_specs=[pl.BlockSpec(memory_space=pltpu.VMEM)] * 12
-        + [pl.BlockSpec(memory_space=pl.ANY)] * 6,
         out_shape=[jax.ShapeDtypeStruct((576, 256), F32)]
         + [jax.ShapeDtypeStruct(s, BF) for s in shapes],
         scratch_shapes=[
@@ -785,14 +765,8 @@
             pltpu.VMEM((4, 8, LANES), F32),
             pltpu.VMEM((4, 128, LANES), F32),
             pltpu.VMEM((12, ROWS, 128), BF),
-            pltpu.VMEM((512, 256), BF),
-            pltpu.VMEM((1024, 512), BF),
-            pltpu.VMEM((512, 1536), BF),
-            pltpu.VMEM((HEADS3, ROWS, LANES), F32),
-            pltpu.VMEM((512, 512), BF),
-            pltpu.SemaphoreType.DMA((6,)),
         ],
-        compiler_params=params(28),
+        compiler_params=params(24),
         cost_estimate=cost(9),
     )(*operands)
 

time: 56.5 us -> 55.8 us (0.988)
  Pallas kernels: 31.9 us -> 31.2 us
    pallas_call x1, Pallas kernels: 7.66 us -> 6.93 us  [middle(): pl.pallas_call(middle_kernel, out_shape=[jax.ShapeDtypeStruct((576, 256),...]
  transfers between devices with their start and end apart: 10 -> 10, of which waited for: 1 -> 1; matrix products, arithmetic and copies ran while one was open for 1% -> 1% of each run, Pallas kernels for 41% -> 42%
where the time goes in v1:
time: 55.8 us; the launch traced here: 55.6 us
  Pallas kernels  31.2 us (56%)
  starting transfers between devices  17.9 us (32%)
  waiting for transfers between devices  2.94 us (5%)
  local copies, waits for them, and re-layouts  2.36 us (4%)
  between operations  1.25 us (2%)
    ppermute x10, starting transfers between devices, send(): return lax.ppermute(values, tuple(axes), pairs)  17.9 us
    pallas_call x2, Pallas kernels, back(): pl.pallas_call(functools.partial(back_kernel, late), out_shape=[jax.Shape...  10.3 us
    pallas_call x2, Pallas kernels, front(): pl.pallas_call(functools.partial(front_kernel, late), out_shape=[jax.Shap...  7.73 us
    pallas_call x1, Pallas kernels, middle(): pl.pallas_call(middle_kernel, out_shape=[jax.ShapeDtypeStruct((576, 256),...  6.93 us
    ppermute x10, waiting for transfers between devices, send(): return lax.ppermute(values, tuple(axes), pairs)  2.94 us
    pallas_call x4, Pallas kernels, merge_call(): pl.pallas_call(kernel, out_shape=[jax.ShapeDtypeStruct(shape, kind) for s...  2.2 us
    pallas_call x1, Pallas kernels, prepare(): pl.pallas_call(prepare_kernel, out_shape=(jax.ShapeDtypeStruct((HEADS1, R...  1.68 us
    unnamed x34, local copies, waits for them, and re-layouts  1.46 us
  transfers between devices with their start and end apart: 10, of which 1 were waited for; matrix products, arithmetic and copies ran while one was open for 1% of the time, Pallas kernels for 42%

profile of v1, /device:TPU:0, one launch (start us, length us, event | category | flops | bytes accessed | tf_op | source)
XLA Modules:
  0.0 55.6 jit_solution(9443584613402679755)
XLA Ops:
  0.6 1.3 %copy.38.tok_ref.refs_0_ = bf16[4,28,28,128]{3,2,1,0:T(8,128)(2,1)S(1)} copy(bf16[4,28,28,128]{3,0,2,1:T(4,128)(2,1)} %param.17) | data formatting | bytes 1605632 | tf_op args[0]
  2.1 0.2 copy.64
  2.3 3.0 %collective-permute-start = (bf16[14,28,2,128]{3,2,1,0:T(2,128)(2,1)S(1)}, bf16[14,28,2,128]{3,2,1,0:T(2,128)(2,1)S(1)}, u32[]{:S(2)}, u32[]{:S(2)}) collective-permute-start(bf16[14,28,2,128]{3,2,1,0:T(2,128)(2,1)S(1)} %bitcast.57), channel_id=1, source_target_pairs={{0,2},{2,0},{1,3},{3,1},{4,6},{6,4},{5,7},{7,5},{8,10},{10,8},{9,1... | collective-permute-start | bytes 602120 | tf_op jit(solution)/shard_map/ppermute | solution.py:869
  5.7 5.1 %collective-permute-start.3 = (bf16[2,6,28,128]{3,2,1,0:T(8,128)(2,1)S(1)}, bf16[2,6,28,128]{3,2,1,0:T(8,128)(2,1)S(1)}, u32[]{:S(2)}, u32[]{:S(2)}) collective-permute-start(bf16[2,6,28,128]{3,2,1,0:T(8,128)(2,1)S(1)} %get-tuple-element.73), channel_id=1, source_target_pairs={{0,28},{4,0},{8,4},{12,8},{16,12},{20,16},{24,20},{28,24},{1,29},{... | collective-permute-start | bytes 258056 | tf_op jit(solution)/shard_map/ppermute | solution.py:869
  10.7 1.4 %collective-permute-start.4 = (bf16[2,6,28,128]{3,2,1,0:T(8,128)(2,1)S(1)}, bf16[2,6,28,128]{3,2,1,0:T(8,128)(2,1)S(1)}, u32[]{:S(2)}, u32[]{:S(2)}) collective-permute-start(bf16[2,6,28,128]{3,2,1,0:T(8,128)(2,1)S(1)} %get-tuple-element.74), channel_id=1, source_target_pairs={{0,30},{2,28},{4,2},{6,0},{8,6},{10,4},{12,10},{14,8},{16,14},{18,... | collective-permute-start | bytes 258056 | tf_op jit(solution)/shard_map/ppermute | solution.py:869
  12.3 1.7 %shard_map.177 = (f32[4,224,256]{2,1,0:T(8,128)S(1)}, f32[7,192,128]{2,1,0:T(8,128)S(1)}, f32[16,1,256]{2,1,0:T(1,128)S(1)}, f32[1,256]{1,0:T(1,128)S(1)}, f32[1...) custom-call(f32[4,1183]{1,0:T(4,128)S(1)} %bitcast.48, f32[16,1183]{1,0:T(8,128)S(1)} %bitcast.46, ...), custom_call_target="tpu_custom_call" | custom-call | flops 1650000000 | bytes 1500000 | tf_op jit(solution)/shard_map/pallas_call | solution.py:267
  14.0 3.9 %shard_map.178 = (bf16[4,9,28,128]{3,2,1,0:T(8,128)(2,1)S(1)}, bf16[4,5,28,128]{3,2,1,0:T(8,128)(2,1)S(1)}, f32[16,112,256]{2,1,0:T(8,128)S(1)}, bf16[8,224,128]...) custom-call(bf16[4,28,28,128]{3,2,1,0:T(8,128)(2,1)S(1)} %copy.38.to, ...), custom_call_target="tpu_custom_call" | custom-call | flops 5059999744 | bytes 4600000 | tf_op jit(solution)/shard_map/pallas_call | solution.py:437
  17.9 0.4 shard_map.179
  18.4 2.5 %collective-permute-start.1 = (bf16[4,5,28,128]{3,2,1,0:T(8,128)(2,1)S(1)}, bf16[4,5,28,128]{3,2,1,0:T(8,128)(2,1)S(1)}, u32[]{:S(2)}, u32[]{:S(2)}) collective-permute-start(bf16[4,5,28,128]{3,2,1,0:T(8,128)(2,1)S(1)} %get-tuple-element.68), channel_id=1, source_target_pairs={{0,28},{4,0},{8,4},{12,8},{16,12},{20,16},{24,20},{28,24},{1,29},{... | collective-permute-start | bytes 430088 | tf_op jit(solution)/shard_map/ppermute | solution.py:869
  21.0 3.9 %shard_map.181 = (bf16[4,14,28,128]{3,2,1,0:T(8,128)(2,1)S(1)}, f32[16,112,256]{2,1,0:T(8,128)S(1)}, bf16[8,224,128]{2,1,0:T(8,128)(2,1)S(1)}, bf16[8,224,256]{2...) custom-call(bf16[4,28,28,128]{3,2,1,0:T(8,128)(2,1)S(1)} %copy.38.to, ...), custom_call_target="tpu_custom_call" | custom-call | flops 5059999744 | bytes 4600000 | tf_op jit(solution)/shard_map/pallas_call | solution.py:437
  24.9 0.6 %shard_map.182 = (f32[576,256]{1,0:T(8,128)S(1)}, f32[576,512]{1,0:T(8,128)S(1)}, f32[576,128]{1,0:T(8,128)S(1)}) custom-call(bf16[4,5,28,128]{3,2,1,0:T(8,128)(2,1)S(1)} %get-tuple-element.71.resA_ref, bf16[4,14,28,128]{3,2,1,0:T(8,128)(2,1)S(1)} %get-tuple-element.75.resB_ref, f32[1,512]{1,0:T(1,128)S(1)} %bitcast.42, bf16[512,256]{1,0:T(8,128)(2,1)S(1)} %copy-done), custom_call_target="tpu_custom_call" | custom-call | flops 110000000 | bytes 100000 | tf_op jit(solution)/shard_map/pallas_call | solution.py:621
  25.6 6.9 %shard_map.183 = (f32[576,256]{1,0:T(8,128)S(1)}, bf16[4,28,128]{2,1,0:T(8,128)(2,1)S(1)}, bf16[4,5,28,128]{3,2,1,0:T(8,128)(2,1)S(1)}, bf16[2,4,28,128]{3,2,1,0...) custom-call(f32[576,256]{1,0:T(8,128)S(1)} %get-tuple-element.77.merged_ref, ...), custom_call_target="tpu_custom_call" | custom-call | flops 9900000256 | bytes 9000000 | tf_op jit(solution)/shard_map/pallas_call | solution.py:748
  32.5 1.1 %collective-permute-start.5 = (bf16[4,5,28,128]{3,2,1,0:T(8,128)(2,1)S(1)}, bf16[4,5,28,128]{3,2,1,0:T(8,128)(2,1)S(1)}, u32[]{:S(2)}, u32[]{:S(2)}) collective-permute-start(bf16[4,5,28,128]{3,2,1,0:T(8,128)(2,1)S(1)} %get-tuple-element.83), channel_id=1, source_target_pairs={{0,4},{4,8},{8,12},{12,16},{16,20},{20,24},{24,28},{28,0},{1,5},{5... | collective-permute-start | bytes 430088 | tf_op jit(solution)/shard_map/ppermute | solution.py:869
  33.6 0.7 %shard_map.184 = (bf16[4,5,28,128]{3,2,1,0:T(8,128)(2,1)S(1)}, bf16[4,14,28,128]{3,2,1,0:T(8,128)(2,1)S(1)}) custom-call(f32[576,256]{1,0:T(8,128)S(1)} %get-tuple-element.84.grad_ref, bf16[4,28,128]{2,1,0:T(8,128)(2,1)S(1)} %get-tuple-element.85.d30_ref, f32[576,512]{1,0:T(8,128)S(1)} %get-tuple-element.86.xhat_ref, ...), custom_call_target="tpu_custom_call" | custom-call | flops 1100000000 | bytes 1000000 | tf_op jit(solution)/shard_map/pallas_call | solution.py:621
  34.3 5.2 %shard_map.185 = (bf16[2,11,28,128]{3,2,1,0:T(8,128)(2,1)S(1)}, bf16[2,15,28,128]{3,2,1,0:T(8,128)(2,1)S(1)}, bf16[4,6,28,128]{3,2,1,0:T(8,128)(2,1)S(1)}) custom-call(bf16[4,14,28,128]{3,2,1,0:T(8,128)(2,1)S(1)} %get-tuple-element.88.refs_0_, bf16[2,7,28,128]{3,2,1,0:T(8,128)(2,1)S(1)} %get-tuple-element.89.refs_1_, ...), custom_call_target="tpu_custom_call" | custom-call | flops 6049999872 | bytes 5500000 | tf_op jit(solution)/shard_map/pallas_call | solution.py:515
  39.6 0.8 %collective-permute-start.7 = (bf16[15,28,2,128]{3,2,1,0:T(2,128)(2,1)S(1)}, bf16[15,28,2,128]{3,2,1,0:T(2,128)(2,1)S(1)}, u32[]{:S(2)}, u32[]{:S(2)}) collective-permute-start(bf16[15,28,2,128]{3,2,1,0:T(2,128)(2,1)S(1)} %bitcast.56), channel_id=1, source_target_pairs={{0,2},{2,0},{1,3},{3,1},{4,6},{6,4},{5,7},{7,5},{8,10},{10,8},{9,1... | collective-permute-start | bytes 645128 | tf_op jit(solution)/shard_map/ppermute | solution.py:869
  40.4 1.2 %collective-permute-start.8 = (bf16[4,6,28,128]{3,2,1,0:T(8,128)(2,1)S(1)}, bf16[4,6,28,128]{3,2,1,0:T(8,128)(2,1)S(1)}, u32[]{:S(2)}, u32[]{:S(2)}) collective-permute-start(bf16[4,6,28,128]{3,2,1,0:T(8,128)(2,1)S(1)} %get-tuple-element.110), channel_id=1, source_target_pairs={{0,4},{4,8},{8,12},{12,16},{16,20},{20,24},{24,28},{28,0},{1,5},{5... | collective-permute-start | bytes 516104 | tf_op jit(solution)/shard_map/ppermute | solution.py:869
  41.6 0.4 shard_map.186.refs_0_
  42.1 5.2 %shard_map.187 = (bf16[2,14,28,128]{3,2,1,0:T(8,128)(2,1)S(1)}, bf16[2,14,28,128]{3,2,1,0:T(8,128)(2,1)S(1)}) custom-call(bf16[4,9,28,128]{3,2,1,0:T(8,128)(2,1)S(1)} %shard_map.186.refs_0_, bf16[4,5,28,128]{3,2,1,0:T(8,128)(2,1)S(1)} %get-tuple-element.101.refs_1_, f32[1,128]{1,0:T(1,128)S(1)} %bitcast.54, bf16[128,384]{1,0:T(8,128)(2,1)S(1)} %copy-done.5, ...), custom_call_target="tpu_custom_call" | custom-call | flops 6049999872 | bytes 5500000 | tf_op jit(solution)/shard_map/pallas_call | solution.py:515
  47.5 1.5 %collective-permute-start.6 = (bf16[14,28,2,128]{3,2,1,0:T(2,128)(2,1)S(1)}, bf16[14,28,2,128]{3,2,1,0:T(2,128)(2,1)S(1)}, u32[]{:S(2)}, u32[]{:S(2)}) collective-permute-start(bf16[14,28,2,128]{3,2,1,0:T(2,128)(2,1)S(1)} %bitcast.58), channel_id=1, source_target_pairs={{0,2},{2,0},{1,3},{3,1},{4,6},{6,4},{5,7},{7,5},{8,10},{10,8},{9,1... | collective-permute-start | bytes 602120 | tf_op jit(solution)/shard_map/ppermute | solution.py:869
  49.0 1.2 %collective-permute-start.9 = (bf16[2,6,28,128]{3,2,1,0:T(8,128)(2,1)S(1)}, bf16[2,6,28,128]{3,2,1,0:T(8,128)(2,1)S(1)}, u32[]{:S(2)}, u32[]{:S(2)}) collective-permute-start(bf16[2,6,28,128]{3,2,1,0:T(8,128)(2,1)S(1)} %slice.3), channel_id=1, source_target_pairs={{0,2},{2,0},{1,3},{3,1},{4,6},{6,4},{5,7},{7,5},{8,10},{10,8},{9,1... | collective-permute-start | bytes 258056 | tf_op jit(solution)/shard_map/ppermute | solution.py:869
  50.2 1.2 %shard_map.188 = (bf16[28,28,4,128]{3,2,1,0:T(4,128)(2,1)}, bf16[7,7,4,512]{3,2,1,0:T(4,128)(2,1)}) custom-call(bf16[2,15,28,128]{3,2,1,0:T(8,128)(2,1)S(1)} %bitcast.38, bf16[2,11,28,128]{3,2,1,0:T(8,128)(2,1)S(1)} %get-tuple-element.114.own_ref, bf16[2,4,28,128]{3,2,1,0:T(8,128)(2,1)S(1)} %get-tuple-element.115.so_ref), custom_call_target="tpu_custom_call" | custom-call | flops 2200000000 | bytes 2000000 | tf_op jit(solution)/shard_map/pallas_call | solution.py:794
  51.4 2.9 %collective-permute-done.9.dg_ref = bf16[2,6,28,128]{3,2,1,0:T(8,128)(2,1)S(1)} collective-permute-done((bf16[2,6,28,128]{3,2,1,0:T(8,128)(2,1)S(1)}, bf16[2,6,28,128]{3,2,1,0:T(8,128)(2,1)S(1)}, u32[]{:S(2)}, u32[]{:S(2)}) %collective-permute-start.9) | collective-permute-done | bytes 86048 | tf_op jit(solution)/shard_map/ppermute | solution.py:869
  54.3 1.1 %shard_map.189 = (bf16[28,28,4,128]{3,2,1,0:T(4,128)(2,1)}, bf16[7,7,4,512]{3,2,1,0:T(4,128)(2,1)}) custom-call(bf16[28,28,4,128]{3,2,1,0:T(4,128)(2,1)} %get-tuple-element.117.grad_hbm, bf16[7,7,4,512]{3,2,1,0:T(4,128)(2,1)} %get-tuple-element.118.section_hbm, bf16[2,14,28,128]{3,2,1,0:T(8,128)(2,1)S(1)} %bitcast.40, ...), custom_call_target="tpu_custom_call", output_to_operand_aliasing={{0}: (0, {}), {1}: (1, {})} | custom-call | flops 1100000000 | bytes 1000000 | tf_op jit(solution)/shard_map/pallas_call | solution.py:829
  (54 shorter events, 1.0 us)
Async XLA Ops:
  0.6 4.7 %copy-start.14 = (bf16[4,7,7,512]{3,0,2,1:T(4,128)(2,1)S(1)}, bf16[4,7,7,512]{3,0,2,1:T(4,128)(2,1)}, u32[]{:S(2)}) copy-start(bf16[4,7,7,512]{3,0,2,1:T(4,128)(2,1)} %param.32) | copy-start | bytes 602116
  2.0 10.2 %copy-start.15 = (s32[4,7,7]{2,0,1:T(4,128)S(1)}, s32[4,7,7]{2,0,1:T(4,128)}, u32[]{:S(2)}) copy-start(s32[4,7,7]{2,0,1:T(4,128)} %param.19) | copy-start | bytes 2356
  2.0 10.2 %copy-start.6 = (f32[1183,16]{0,1:T(8,128)S(1)}, f32[1183,16]{0,1:T(8,128)}, u32[]{:S(2)}) copy-start(f32[1183,16]{0,1:T(8,128)} %param.31) | copy-start | bytes 227140
  2.0 10.2 %copy-start.7 = (s32[4,28,28]{2,0,1:T(4,128)S(1)}, s32[4,28,28]{2,0,1:T(4,128)}, u32[]{:S(2)}) copy-start(s32[4,28,28]{2,0,1:T(4,128)} %param.18) | copy-start | bytes 37636
  2.0 10.2 %copy-start.9 = (f32[1183,4]{0,1:T(4,128)S(1)}, f32[1183,4]{0,1:T(4,128)}, u32[]{:S(2)}) copy-start(f32[1183,4]{0,1:T(4,128)} %param.23) | copy-start | bytes 56788
  2.0 10.2 %copy-start.13 = (bf16[256,1024]{1,0:T(8,128)(2,1)S(1)}, bf16[256,1024]{1,0:T(8,128)(2,1)}, u32[]{:S(2)}) copy-start(bf16[256,1024]{1,0:T(8,128)(2,1)} %constant.2.clone.s_ref) | copy-start | bytes 1572868
  2.3 11.7 %collective-permute-start = (bf16[14,28,2,128]{3,2,1,0:T(2,128)(2,1)S(1)}, bf16[14,28,2,128]{3,2,1,0:T(2,128)(2,1)S(1)}, u32[]{:S(2)}, u32[]{:S(2)}) collective-permute-start(bf16[14,28,2,128]{3,2,1,0:T(2,128)(2,1)S(1)} %bitcast.57), channel_id=1, source_target_pairs={{0,2},{2,0},{1,3},{3,1},{4,6},{6,4},{5,7},{7,5},{8,10},{10,8},{9,1... | collective-permute-start | bytes 602120 | tf_op jit(solution)/shard_map/ppermute | solution.py:869
  5.6 15.3 %collective-permute-start.2 = (bf16[15,28,2,128]{3,2,1,0:T(2,128)(2,1)S(1)}, bf16[15,28,2,128]{3,2,1,0:T(2,128)(2,1)S(1)}, u32[]{:S(2)}, u32[]{:S(2)}) collective-permute-start(bf16[15,28,2,128]{3,2,1,0:T(2,128)(2,1)S(1)} %bitcast.55), channel_id=1, source_target_pairs={{0,2},{2,0},{1,3},{3,1},{4,6},{6,4},{5,7},{7,5},{8,10},{10,8},{9,1... | collective-permute-start | bytes 645128 | tf_op jit(solution)/shard_map/ppermute | solution.py:869
  5.7 15.3 %collective-permute-start.3 = (bf16[2,6,28,128]{3,2,1,0:T(8,128)(2,1)S(1)}, bf16[2,6,28,128]{3,2,1,0:T(8,128)(2,1)S(1)}, u32[]{:S(2)}, u32[]{:S(2)}) collective-permute-start(bf16[2,6,28,128]{3,2,1,0:T(8,128)(2,1)S(1)} %get-tuple-element.73), channel_id=1, source_target_pairs={{0,28},{4,0},{8,4},{12,8},{16,12},{20,16},{24,20},{28,24},{1,29},{... | collective-permute-start | bytes 258056 | tf_op jit(solution)/shard_map/ppermute | solution.py:869
  10.7 10.2 %collective-permute-start.4 = (bf16[2,6,28,128]{3,2,1,0:T(8,128)(2,1)S(1)}, bf16[2,6,28,128]{3,2,1,0:T(8,128)(2,1)S(1)}, u32[]{:S(2)}, u32[]{:S(2)}) collective-permute-start(bf16[2,6,28,128]{3,2,1,0:T(8,128)(2,1)S(1)} %get-tuple-element.74), channel_id=1, source_target_pairs={{0,30},{2,28},{4,2},{6,0},{8,6},{10,4},{12,10},{14,8},{16,14},{18,... | collective-permute-start | bytes 258056 | tf_op jit(solution)/shard_map/ppermute | solution.py:869
  12.2 1.8 %copy-start.5 = (bf16[128,384]{1,0:T(8,128)(2,1)S(1)}, bf16[128,384]{1,0:T(8,128)(2,1)}, u32[]{:S(2)}) copy-start(bf16[128,384]{1,0:T(8,128)(2,1)} %refs_3_.3) | copy-start | bytes 294916
  14.0 3.9 %copy-start = (bf16[512,256]{1,0:T(8,128)(2,1)S(1)}, bf16[512,256]{1,0:T(8,128)(2,1)}, u32[]{:S(2)}) copy-start(bf16[512,256]{1,0:T(8,128)(2,1)} %weight_ref.7) | copy-start | bytes 786436
  14.0 3.9 %copy-start.1 = (f32[512]{0:T(512)S(1)}, f32[512]{0:T(512)}, u32[]{:S(2)}) copy-start(f32[512]{0:T(512)} %param.24) | copy-start | bytes 6148
  18.4 7.1 %collective-permute-start.1 = (bf16[4,5,28,128]{3,2,1,0:T(8,128)(2,1)S(1)}, bf16[4,5,28,128]{3,2,1,0:T(8,128)(2,1)S(1)}, u32[]{:S(2)}, u32[]{:S(2)}) collective-permute-start(bf16[4,5,28,128]{3,2,1,0:T(8,128)(2,1)S(1)} %get-tuple-element.68), channel_id=1, source_target_pairs={{0,28},{4,0},{8,4},{12,8},{16,12},{20,16},{24,20},{28,24},{1,29},{... | collective-permute-start | bytes 430088 | tf_op jit(solution)/shard_map/ppermute | solution.py:869
  20.9 4.6 %copy-start.2 = (bf16[512,1536]{1,0:T(8,128)(2,1)S(1)}, bf16[512,1536]{1,0:T(8,128)(2,1)}, u32[]{:S(2)}) copy-start(bf16[512,1536]{1,0:T(8,128)(2,1)} %p3_ref.1) | copy-start | bytes 4718596
  21.0 4.6 %copy-start.3 = (bf16[1024,512]{1,0:T(8,128)(2,1)S(1)}, bf16[1024,512]{1,0:T(8,128)(2,1)}, u32[]{:S(2)}) copy-start(bf16[1024,512]{1,0:T(8,128)(2,1)} %mw2_ref.1) | copy-start | bytes 3145732
  21.0 4.6 %copy-start.4 = (bf16[512,512]{1,0:T(8,128)(2,1)S(1)}, bf16[512,512]{1,0:T(8,128)(2,1)}, u32[]{:S(2)}) copy-start(bf16[512,512]{1,0:T(8,128)(2,1)} %ow3_ref.1) | copy-start | bytes 1572868
  21.0 4.6 %copy-start.10 = (f32[1024]{0:T(1024)S(1)}, f32[1024]{0:T(1024)}, u32[]{:S(2)}) copy-start(f32[1024]{0:T(1024)} %param.26) | copy-start | bytes 12292
  21.0 4.6 %copy-start.11 = (f32[512]{0:T(512)S(1)}, f32[512]{0:T(512)}, u32[]{:S(2)}) copy-start(f32[512]{0:T(512)} %param.28) | copy-start | bytes 6148
  32.5 9.1 %collective-permute-start.5 = (bf16[4,5,28,128]{3,2,1,0:T(8,128)(2,1)S(1)}, bf16[4,5,28,128]{3,2,1,0:T(8,128)(2,1)S(1)}, u32[]{:S(2)}, u32[]{:S(2)}) collective-permute-start(bf16[4,5,28,128]{3,2,1,0:T(8,128)(2,1)S(1)} %get-tuple-element.83), channel_id=1, source_target_pairs={{0,4},{4,8},{8,12},{12,16},{16,20},{20,24},{24,28},{28,0},{1,5},{5... | collective-permute-start | bytes 430088 | tf_op jit(solution)/shard_map/ppermute | solution.py:869
  39.6 9.3 %collective-permute-start.7 = (bf16[15,28,2,128]{3,2,1,0:T(2,128)(2,1)S(1)}, bf16[15,28,2,128]{3,2,1,0:T(2,128)(2,1)S(1)}, u32[]{:S(2)}, u32[]{:S(2)}) collective-permute-start(bf16[15,28,2,128]{3,2,1,0:T(2,128)(2,1)S(1)} %bitcast.56), channel_id=1, source_target_pairs={{0,2},{2,0},{1,3},{3,1},{4,6},{6,4},{5,7},{7,5},{8,10},{10,8},{9,1... | collective-permute-start | bytes 645128 | tf_op jit(solution)/shard_map/ppermute | solution.py:869
  40.4 8.5 %collective-permute-start.8 = (bf16[4,6,28,128]{3,2,1,0:T(8,128)(2,1)S(1)}, bf16[4,6,28,128]{3,2,1,0:T(8,128)(2,1)S(1)}, u32[]{:S(2)}, u32[]{:S(2)}) collective-permute-start(bf16[4,6,28,128]{3,2,1,0:T(8,128)(2,1)S(1)} %get-tuple-element.110), channel_id=1, source_target_pairs={{0,4},{4,8},{8,12},{12,16},{16,20},{20,24},{24,28},{28,0},{1,5},{5... | collective-permute-start | bytes 516104 | tf_op jit(solution)/shard_map/ppermute | solution.py:869
  47.5 6.8 %collective-permute-start.6 = (bf16[14,28,2,128]{3,2,1,0:T(2,128)(2,1)S(1)}, bf16[14,28,2,128]{3,2,1,0:T(2,128)(2,1)S(1)}, u32[]{:S(2)}, u32[]{:S(2)}) collective-permute-start(bf16[14,28,2,128]{3,2,1,0:T(2,128)(2,1)S(1)} %bitcast.58), channel_id=1, source_target_pairs={{0,2},{2,0},{1,3},{3,1},{4,6},{6,4},{5,7},{7,5},{8,10},{10,8},{9,1... | collective-permute-start | bytes 602120 | tf_op jit(solution)/shard_map/ppermute | solution.py:869
  49.0 5.3 %collective-permute-start.9 = (bf16[2,6,28,128]{3,2,1,0:T(8,128)(2,1)S(1)}, bf16[2,6,28,128]{3,2,1,0:T(8,128)(2,1)S(1)}, u32[]{:S(2)}, u32[]{:S(2)}) collective-permute-start(bf16[2,6,28,128]{3,2,1,0:T(8,128)(2,1)S(1)} %slice.3), channel_id=1, source_target_pairs={{0,2},{2,0},{1,3},{3,1},{4,6},{6,4},{5,7},{7,5},{8,10},{10,8},{9,1... | collective-permute-start | bytes 258056 | tf_op jit(solution)/shard_map/ppermute | solution.py:869
  (2 other events, 3.5 us)

commit v2 on v1

--- a/solution.py
+++ b/solution.py
@@ -89,11 +89,9 @@
     return jnp.where(jnp.concatenate([column, column], 1) == row, 0.0, GONE).astype(F32)
 
 
-def stagger(pending):
-    pending, active = list(pending), []
-    while pending or active:
-        if pending:
-            active.append(pending.pop(0))
+def lockstep(active):
+    active = list(active)
+    while active:
         active = [g for g in active if next(g, "end") is None]
 
 
@@ -502,7 +500,7 @@
         xhat, rstd = normalise(xw_ref[w].astype(F32))
         win[w] = dr + normalise_back(dn * gain_ref[...], xhat, rstd)
 
-    stagger(window(step * PER_STEP + u) for u in range(PER_STEP))
+    lockstep(window(step * PER_STEP + u) for u in range(PER_STEP))
     return carry
 
 
@@ -721,7 +719,7 @@
             v_s[g], qT_s[g], kT_s[g], oT_s[g], doT_s[g], inv_s[g], lambda h: probs_s[g * 4 + h]
         )
 
-    stagger(group_back(g) for g in range(4))
+    lockstep(group_back(g) for g in range(4))
     dpacked = jnp.concatenate([dqkv_s[i] for i in range(12)], 1)
     dn3 = dot_nt(dpacked, p3_ref[...])
     dm2 = cot + normalise_back(dn3 * g3_ref[...], xhat3, rstd3)
@@ -812,15 +810,20 @@
         high = corner[t % 2, 3:6].astype(F32)
         for g in range(4):
             narrow[g, :, pl.ds(t, 7, stride=4), :] = high[:, 7 * g : 7 * g + 7]
-    for i in range(17):
+    for i in range(8):
         rows[i] = wide[i].reshape(28, 4, 128).astype(BF)
-    copy = pltpu.make_async_copy(rows, grad_out.at[0:17], sems.at[0])
+    start = pltpu.make_async_copy(rows.at[0:8], grad_out.at[0:8], sems.at[2])
+    start.start()
+    for i in range(8, 17):
+        rows[i] = wide[i].reshape(28, 4, 128).astype(BF)
+    copy = pltpu.make_async_copy(rows.at[8:17], grad_out.at[8:17], sems.at[0])
     copy.start()
     for i in range(3):
         row = jnp.concatenate([narrow[g, i] for g in range(4)], 1)
         section_rows[i] = row.reshape(7, 4, 512).astype(BF)
     other = pltpu.make_async_copy(section_rows, section_out.at[0:3], sems.at[1])
     other.start()
+    start.wait()
     copy.wait()
     other.wait()
 
@@ -837,7 +840,7 @@
             pltpu.VMEM((4, 3, 28, 128), F32),
             pltpu.VMEM((17, 28, 4, 128), BF),
             pltpu.VMEM((3, 7, 4, 512), BF),
-            pltpu.SemaphoreType.DMA((2,)),
+            pltpu.SemaphoreType.DMA((3,)),
         ],
         input_output_aliases={0: 0, 1: 1},
         compiler_params=params(),

time: 55.8 us -> 55.7 us (level)
  no operation moved by 1% of the time
where the time goes in v2:
time: 55.7 us; the launch traced here: 55.6 us
  Pallas kernels  31.2 us (56%)
  starting transfers between devices  17.9 us (32%)
  waiting for transfers between devices  2.96 us (5%)
  local copies, waits for them, and re-layouts  2.36 us (4%)
  between operations  1.24 us (2%)
    ppermute x10, starting transfers between devices, send(): return lax.ppermute(values, tuple(axes), pairs)  17.9 us
    pallas_call x2, Pallas kernels, back(): pl.pallas_call(functools.partial(back_kernel, late), out_shape=[jax.Shape...  10.3 us
    pallas_call x2, Pallas kernels, front(): pl.pallas_call(functools.partial(front_kernel, late), out_shape=[jax.Shap...  7.73 us
    pallas_call x1, Pallas kernels, middle(): pl.pallas_call(middle_kernel, out_shape=[jax.ShapeDtypeStruct((576, 256),...  6.92 us
    ppermute x10, waiting for transfers between devices, send(): return lax.ppermute(values, tuple(axes), pairs)  2.96 us
    pallas_call x4, Pallas kernels, merge_call(): pl.pallas_call(kernel, out_shape=[jax.ShapeDtypeStruct(shape, kind) for s...  2.2 us
    pallas_call x1, Pallas kernels, prepare(): pl.pallas_call(prepare_kernel, out_shape=(jax.ShapeDtypeStruct((HEADS1, R...  1.68 us
    unnamed x34, local copies, waits for them, and re-layouts  1.46 us
  transfers between devices with their start and end apart: 10, of which 1 were waited for; matrix products, arithmetic and copies ran while one was open for 1% of the time, Pallas kernels for 42%

profile of v2, /device:TPU:0, one launch (start us, length us, event | category | flops | bytes accessed | tf_op | source)
XLA Modules:
  0.0 55.6 jit_solution(16590358770552556158)
XLA Ops:
  0.6 1.3 %copy.38.tok_ref.refs_0_ = bf16[4,28,28,128]{3,2,1,0:T(8,128)(2,1)S(1)} copy(bf16[4,28,28,128]{3,0,2,1:T(4,128)(2,1)} %param.17) | data formatting | bytes 1605632 | tf_op args[0]
  2.1 0.2 copy.64
  2.3 3.0 %collective-permute-start = (bf16[14,28,2,128]{3,2,1,0:T(2,128)(2,1)S(1)}, bf16[14,28,2,128]{3,2,1,0:T(2,128)(2,1)S(1)}, u32[]{:S(2)}, u32[]{:S(2)}) collective-permute-start(bf16[14,28,2,128]{3,2,1,0:T(2,128)(2,1)S(1)} %bitcast.57), channel_id=1, source_target_pairs={{0,2},{2,0},{1,3},{3,1},{4,6},{6,4},{5,7},{7,5},{8,10},{10,8},{9,1... | collective-permute-start | bytes 602120 | tf_op jit(solution)/shard_map/ppermute | solution.py:872
  5.7 5.1 %collective-permute-start.3 = (bf16[2,6,28,128]{3,2,1,0:T(8,128)(2,1)S(1)}, bf16[2,6,28,128]{3,2,1,0:T(8,128)(2,1)S(1)}, u32[]{:S(2)}, u32[]{:S(2)}) collective-permute-start(bf16[2,6,28,128]{3,2,1,0:T(8,128)(2,1)S(1)} %get-tuple-element.73), channel_id=1, source_target_pairs={{0,28},{4,0},{8,4},{12,8},{16,12},{20,16},{24,20},{28,24},{1,29},{... | collective-permute-start | bytes 258056 | tf_op jit(solution)/shard_map/ppermute | solution.py:872
  10.7 1.4 %collective-permute-start.4 = (bf16[2,6,28,128]{3,2,1,0:T(8,128)(2,1)S(1)}, bf16[2,6,28,128]{3,2,1,0:T(8,128)(2,1)S(1)}, u32[]{:S(2)}, u32[]{:S(2)}) collective-permute-start(bf16[2,6,28,128]{3,2,1,0:T(8,128)(2,1)S(1)} %get-tuple-element.74), channel_id=1, source_target_pairs={{0,30},{2,28},{4,2},{6,0},{8,6},{10,4},{12,10},{14,8},{16,14},{18,... | collective-permute-start | bytes 258056 | tf_op jit(solution)/shard_map/ppermute | solution.py:872
  12.3 1.7 %shard_map.177 = (f32[4,224,256]{2,1,0:T(8,128)S(1)}, f32[7,192,128]{2,1,0:T(8,128)S(1)}, f32[16,1,256]{2,1,0:T(1,128)S(1)}, f32[1,256]{1,0:T(1,128)S(1)}, f32[1...) custom-call(f32[4,1183]{1,0:T(4,128)S(1)} %bitcast.48, f32[16,1183]{1,0:T(8,128)S(1)} %bitcast.46, ...), custom_call_target="tpu_custom_call" | custom-call | flops 1650000000 | bytes 1500000 | tf_op jit(solution)/shard_map/pallas_call | solution.py:265
  14.0 3.9 %shard_map.178 = (bf16[4,9,28,128]{3,2,1,0:T(8,128)(2,1)S(1)}, bf16[4,5,28,128]{3,2,1,0:T(8,128)(2,1)S(1)}, f32[16,112,256]{2,1,0:T(8,128)S(1)}, bf16[8,224,128]...) custom-call(bf16[4,28,28,128]{3,2,1,0:T(8,128)(2,1)S(1)} %copy.38.to, ...), custom_call_target="tpu_custom_call" | custom-call | flops 5059999744 | bytes 4600000 | tf_op jit(solution)/shard_map/pallas_call | solution.py:435
  17.9 0.4 shard_map.179
  18.4 2.5 %collective-permute-start.1 = (bf16[4,5,28,128]{3,2,1,0:T(8,128)(2,1)S(1)}, bf16[4,5,28,128]{3,2,1,0:T(8,128)(2,1)S(1)}, u32[]{:S(2)}, u32[]{:S(2)}) collective-permute-start(bf16[4,5,28,128]{3,2,1,0:T(8,128)(2,1)S(1)} %get-tuple-element.68), channel_id=1, source_target_pairs={{0,28},{4,0},{8,4},{12,8},{16,12},{20,16},{24,20},{28,24},{1,29},{... | collective-permute-start | bytes 430088 | tf_op jit(solution)/shard_map/ppermute | solution.py:872
  21.0 3.9 %shard_map.181 = (bf16[4,14,28,128]{3,2,1,0:T(8,128)(2,1)S(1)}, f32[16,112,256]{2,1,0:T(8,128)S(1)}, bf16[8,224,128]{2,1,0:T(8,128)(2,1)S(1)}, bf16[8,224,256]{2...) custom-call(bf16[4,28,28,128]{3,2,1,0:T(8,128)(2,1)S(1)} %copy.38.to, ...), custom_call_target="tpu_custom_call" | custom-call | flops 5059999744 | bytes 4600000 | tf_op jit(solution)/shard_map/pallas_call | solution.py:435
  24.9 0.6 %shard_map.182 = (f32[576,256]{1,0:T(8,128)S(1)}, f32[576,512]{1,0:T(8,128)S(1)}, f32[576,128]{1,0:T(8,128)S(1)}) custom-call(bf16[4,5,28,128]{3,2,1,0:T(8,128)(2,1)S(1)} %get-tuple-element.71.resA_ref, bf16[4,14,28,128]{3,2,1,0:T(8,128)(2,1)S(1)} %get-tuple-element.75.resB_ref, f32[1,512]{1,0:T(1,128)S(1)} %bitcast.42, bf16[512,256]{1,0:T(8,128)(2,1)S(1)} %copy-done), custom_call_target="tpu_custom_call" | custom-call | flops 110000000 | bytes 100000 | tf_op jit(solution)/shard_map/pallas_call | solution.py:619
  25.6 6.9 %shard_map.183 = (f32[576,256]{1,0:T(8,128)S(1)}, bf16[4,28,128]{2,1,0:T(8,128)(2,1)S(1)}, bf16[4,5,28,128]{3,2,1,0:T(8,128)(2,1)S(1)}, bf16[2,4,28,128]{3,2,1,0...) custom-call(f32[576,256]{1,0:T(8,128)S(1)} %get-tuple-element.77.merged_ref, ...), custom_call_target="tpu_custom_call" | custom-call | flops 9900000256 | bytes 9000000 | tf_op jit(solution)/shard_map/pallas_call | solution.py:746
  32.5 1.1 %collective-permute-start.5 = (bf16[4,5,28,128]{3,2,1,0:T(8,128)(2,1)S(1)}, bf16[4,5,28,128]{3,2,1,0:T(8,128)(2,1)S(1)}, u32[]{:S(2)}, u32[]{:S(2)}) collective-permute-start(bf16[4,5,28,128]{3,2,1,0:T(8,128)(2,1)S(1)} %get-tuple-element.83), channel_id=1, source_target_pairs={{0,4},{4,8},{8,12},{12,16},{16,20},{20,24},{24,28},{28,0},{1,5},{5... | collective-permute-start | bytes 430088 | tf_op jit(solution)/shard_map/ppermute | solution.py:872
  33.6 0.7 %shard_map.184 = (bf16[4,5,28,128]{3,2,1,0:T(8,128)(2,1)S(1)}, bf16[4,14,28,128]{3,2,1,0:T(8,128)(2,1)S(1)}) custom-call(f32[576,256]{1,0:T(8,128)S(1)} %get-tuple-element.84.grad_ref, bf16[4,28,128]{2,1,0:T(8,128)(2,1)S(1)} %get-tuple-element.85.d30_ref, f32[576,512]{1,0:T(8,128)S(1)} %get-tuple-element.86.xhat_ref, ...), custom_call_target="tpu_custom_call" | custom-call | flops 1100000000 | bytes 1000000 | tf_op jit(solution)/shard_map/pallas_call | solution.py:619
  34.3 5.2 %shard_map.185 = (bf16[2,11,28,128]{3,2,1,0:T(8,128)(2,1)S(1)}, bf16[2,15,28,128]{3,2,1,0:T(8,128)(2,1)S(1)}, bf16[4,6,28,128]{3,2,1,0:T(8,128)(2,1)S(1)}) custom-call(bf16[4,14,28,128]{3,2,1,0:T(8,128)(2,1)S(1)} %get-tuple-element.88.refs_0_, bf16[2,7,28,128]{3,2,1,0:T(8,128)(2,1)S(1)} %get-tuple-element.89.refs_1_, ...), custom_call_target="tpu_custom_call" | custom-call | flops 6049999872 | bytes 5500000 | tf_op jit(solution)/shard_map/pallas_call | solution.py:513
  39.6 0.8 %collective-permute-start.7 = (bf16[15,28,2,128]{3,2,1,0:T(2,128)(2,1)S(1)}, bf16[15,28,2,128]{3,2,1,0:T(2,128)(2,1)S(1)}, u32[]{:S(2)}, u32[]{:S(2)}) collective-permute-start(bf16[15,28,2,128]{3,2,1,0:T(2,128)(2,1)S(1)} %bitcast.56), channel_id=1, source_target_pairs={{0,2},{2,0},{1,3},{3,1},{4,6},{6,4},{5,7},{7,5},{8,10},{10,8},{9,1... | collective-permute-start | bytes 645128 | tf_op jit(solution)/shard_map/ppermute | solution.py:872
  40.4 1.2 %collective-permute-start.8 = (bf16[4,6,28,128]{3,2,1,0:T(8,128)(2,1)S(1)}, bf16[4,6,28,128]{3,2,1,0:T(8,128)(2,1)S(1)}, u32[]{:S(2)}, u32[]{:S(2)}) collective-permute-start(bf16[4,6,28,128]{3,2,1,0:T(8,128)(2,1)S(1)} %get-tuple-element.110), channel_id=1, source_target_pairs={{0,4},{4,8},{8,12},{12,16},{16,20},{20,24},{24,28},{28,0},{1,5},{5... | collective-permute-start | bytes 516104 | tf_op jit(solution)/shard_map/ppermute | solution.py:872
  41.7 0.4 shard_map.186.refs_0_
  42.1 5.2 %shard_map.187 = (bf16[2,14,28,128]{3,2,1,0:T(8,128)(2,1)S(1)}, bf16[2,14,28,128]{3,2,1,0:T(8,128)(2,1)S(1)}) custom-call(bf16[4,9,28,128]{3,2,1,0:T(8,128)(2,1)S(1)} %shard_map.186.refs_0_, bf16[4,5,28,128]{3,2,1,0:T(8,128)(2,1)S(1)} %get-tuple-element.101.refs_1_, f32[1,128]{1,0:T(1,128)S(1)} %bitcast.54, bf16[128,384]{1,0:T(8,128)(2,1)S(1)} %copy-done.5, ...), custom_call_target="tpu_custom_call" | custom-call | flops 6049999872 | bytes 5500000 | tf_op jit(solution)/shard_map/pallas_call | solution.py:513
  47.5 1.5 %collective-permute-start.6 = (bf16[14,28,2,128]{3,2,1,0:T(2,128)(2,1)S(1)}, bf16[14,28,2,128]{3,2,1,0:T(2,128)(2,1)S(1)}, u32[]{:S(2)}, u32[]{:S(2)}) collective-permute-start(bf16[14,28,2,128]{3,2,1,0:T(2,128)(2,1)S(1)} %bitcast.58), channel_id=1, source_target_pairs={{0,2},{2,0},{1,3},{3,1},{4,6},{6,4},{5,7},{7,5},{8,10},{10,8},{9,1... | collective-permute-start | bytes 602120 | tf_op jit(solution)/shard_map/ppermute | solution.py:872
  49.0 1.2 %collective-permute-start.9 = (bf16[2,6,28,128]{3,2,1,0:T(8,128)(2,1)S(1)}, bf16[2,6,28,128]{3,2,1,0:T(8,128)(2,1)S(1)}, u32[]{:S(2)}, u32[]{:S(2)}) collective-permute-start(bf16[2,6,28,128]{3,2,1,0:T(8,128)(2,1)S(1)} %slice.3), channel_id=1, source_target_pairs={{0,2},{2,0},{1,3},{3,1},{4,6},{6,4},{5,7},{7,5},{8,10},{10,8},{9,1... | collective-permute-start | bytes 258056 | tf_op jit(solution)/shard_map/ppermute | solution.py:872
  50.2 1.2 %shard_map.188 = (bf16[28,28,4,128]{3,2,1,0:T(4,128)(2,1)}, bf16[7,7,4,512]{3,2,1,0:T(4,128)(2,1)}) custom-call(bf16[2,15,28,128]{3,2,1,0:T(8,128)(2,1)S(1)} %bitcast.38, bf16[2,11,28,128]{3,2,1,0:T(8,128)(2,1)S(1)} %get-tuple-element.114.own_ref, bf16[2,4,28,128]{3,2,1,0:T(8,128)(2,1)S(1)} %get-tuple-element.115.so_ref), custom_call_target="tpu_custom_call" | custom-call | flops 2200000000 | bytes 2000000 | tf_op jit(solution)/shard_map/pallas_call | solution.py:792
  51.3 2.9 %collective-permute-done.9.dg_ref = bf16[2,6,28,128]{3,2,1,0:T(8,128)(2,1)S(1)} collective-permute-done((bf16[2,6,28,128]{3,2,1,0:T(8,128)(2,1)S(1)}, bf16[2,6,28,128]{3,2,1,0:T(8,128)(2,1)S(1)}, u32[]{:S(2)}, u32[]{:S(2)}) %collective-permute-start.9) | collective-permute-done | bytes 86048 | tf_op jit(solution)/shard_map/ppermute | solution.py:872
  54.3 1.1 %shard_map.189 = (bf16[28,28,4,128]{3,2,1,0:T(4,128)(2,1)}, bf16[7,7,4,512]{3,2,1,0:T(4,128)(2,1)}) custom-call(bf16[28,28,4,128]{3,2,1,0:T(4,128)(2,1)} %get-tuple-element.117.grad_hbm, bf16[7,7,4,512]{3,2,1,0:T(4,128)(2,1)} %get-tuple-element.118.section_hbm, bf16[2,14,28,128]{3,2,1,0:T(8,128)(2,1)S(1)} %bitcast.40, ...), custom_call_target="tpu_custom_call", output_to_operand_aliasing={{0}: (0, {}), {1}: (1, {})} | custom-call | flops 1100000000 | bytes 1000000 | tf_op jit(solution)/shard_map/pallas_call | solution.py:832
  (54 shorter events, 1.0 us)
Async XLA Ops:
  0.6 4.7 %copy-start.14 = (bf16[4,7,7,512]{3,0,2,1:T(4,128)(2,1)S(1)}, bf16[4,7,7,512]{3,0,2,1:T(4,128)(2,1)}, u32[]{:S(2)}) copy-start(bf16[4,7,7,512]{3,0,2,1:T(4,128)(2,1)} %param.32) | copy-start | bytes 602116
  2.0 10.2 %copy-start.15 = (s32[4,7,7]{2,0,1:T(4,128)S(1)}, s32[4,7,7]{2,0,1:T(4,128)}, u32[]{:S(2)}) copy-start(s32[4,7,7]{2,0,1:T(4,128)} %param.19) | copy-start | bytes 2356
  2.0 10.2 %copy-start.6 = (f32[1183,16]{0,1:T(8,128)S(1)}, f32[1183,16]{0,1:T(8,128)}, u32[]{:S(2)}) copy-start(f32[1183,16]{0,1:T(8,128)} %param.31) | copy-start | bytes 227140
  2.0 10.2 %copy-start.7 = (s32[4,28,28]{2,0,1:T(4,128)S(1)}, s32[4,28,28]{2,0,1:T(4,128)}, u32[]{:S(2)}) copy-start(s32[4,28,28]{2,0,1:T(4,128)} %param.18) | copy-start | bytes 37636
  2.0 10.2 %copy-start.9 = (f32[1183,4]{0,1:T(4,128)S(1)}, f32[1183,4]{0,1:T(4,128)}, u32[]{:S(2)}) copy-start(f32[1183,4]{0,1:T(4,128)} %param.23) | copy-start | bytes 56788
  2.0 10.2 %copy-start.13 = (bf16[256,1024]{1,0:T(8,128)(2,1)S(1)}, bf16[256,1024]{1,0:T(8,128)(2,1)}, u32[]{:S(2)}) copy-start(bf16[256,1024]{1,0:T(8,128)(2,1)} %constant.2.clone.s_ref) | copy-start | bytes 1572868
  2.3 11.7 %collective-permute-start = (bf16[14,28,2,128]{3,2,1,0:T(2,128)(2,1)S(1)}, bf16[14,28,2,128]{3,2,1,0:T(2,128)(2,1)S(1)}, u32[]{:S(2)}, u32[]{:S(2)}) collective-permute-start(bf16[14,28,2,128]{3,2,1,0:T(2,128)(2,1)S(1)} %bitcast.57), channel_id=1, source_target_pairs={{0,2},{2,0},{1,3},{3,1},{4,6},{6,4},{5,7},{7,5},{8,10},{10,8},{9,1... | collective-permute-start | bytes 602120 | tf_op jit(solution)/shard_map/ppermute | solution.py:872
  5.6 15.3 %collective-permute-start.2 = (bf16[15,28,2,128]{3,2,1,0:T(2,128)(2,1)S(1)}, bf16[15,28,2,128]{3,2,1,0:T(2,128)(2,1)S(1)}, u32[]{:S(2)}, u32[]{:S(2)}) collective-permute-start(bf16[15,28,2,128]{3,2,1,0:T(2,128)(2,1)S(1)} %bitcast.55), channel_id=1, source_target_pairs={{0,2},{2,0},{1,3},{3,1},{4,6},{6,4},{5,7},{7,5},{8,10},{10,8},{9,1... | collective-permute-start | bytes 645128 | tf_op jit(solution)/shard_map/ppermute | solution.py:872
  5.7 15.3 %collective-permute-start.3 = (bf16[2,6,28,128]{3,2,1,0:T(8,128)(2,1)S(1)}, bf16[2,6,28,128]{3,2,1,0:T(8,128)(2,1)S(1)}, u32[]{:S(2)}, u32[]{:S(2)}) collective-permute-start(bf16[2,6,28,128]{3,2,1,0:T(8,128)(2,1)S(1)} %get-tuple-element.73), channel_id=1, source_target_pairs={{0,28},{4,0},{8,4},{12,8},{16,12},{20,16},{24,20},{28,24},{1,29},{... | collective-permute-start | bytes 258056 | tf_op jit(solution)/shard_map/ppermute | solution.py:872
  10.7 10.2 %collective-permute-start.4 = (bf16[2,6,28,128]{3,2,1,0:T(8,128)(2,1)S(1)}, bf16[2,6,28,128]{3,2,1,0:T(8,128)(2,1)S(1)}, u32[]{:S(2)}, u32[]{:S(2)}) collective-permute-start(bf16[2,6,28,128]{3,2,1,0:T(8,128)(2,1)S(1)} %get-tuple-element.74), channel_id=1, source_target_pairs={{0,30},{2,28},{4,2},{6,0},{8,6},{10,4},{12,10},{14,8},{16,14},{18,... | collective-permute-start | bytes 258056 | tf_op jit(solution)/shard_map/ppermute | solution.py:872
  12.2 1.8 %copy-start.5 = (bf16[128,384]{1,0:T(8,128)(2,1)S(1)}, bf16[128,384]{1,0:T(8,128)(2,1)}, u32[]{:S(2)}) copy-start(bf16[128,384]{1,0:T(8,128)(2,1)} %refs_3_.3) | copy-start | bytes 294916
  14.0 3.9 %copy-start = (bf16[512,256]{1,0:T(8,128)(2,1)S(1)}, bf16[512,256]{1,0:T(8,128)(2,1)}, u32[]{:S(2)}) copy-start(bf16[512,256]{1,0:T(8,128)(2,1)} %weight_ref.7) | copy-start | bytes 786436
  14.0 3.9 %copy-start.1 = (f32[512]{0:T(512)S(1)}, f32[512]{0:T(512)}, u32[]{:S(2)}) copy-start(f32[512]{0:T(512)} %param.24) | copy-start | bytes 6148
  18.4 7.1 %collective-permute-start.1 = (bf16[4,5,28,128]{3,2,1,0:T(8,128)(2,1)S(1)}, bf16[4,5,28,128]{3,2,1,0:T(8,128)(2,1)S(1)}, u32[]{:S(2)}, u32[]{:S(2)}) collective-permute-start(bf16[4,5,28,128]{3,2,1,0:T(8,128)(2,1)S(1)} %get-tuple-element.68), channel_id=1, source_target_pairs={{0,28},{4,0},{8,4},{12,8},{16,12},{20,16},{24,20},{28,24},{1,29},{... | collective-permute-start | bytes 430088 | tf_op jit(solution)/shard_map/ppermute | solution.py:872
  20.9 4.6 %copy-start.2 = (bf16[512,1536]{1,0:T(8,128)(2,1)S(1)}, bf16[512,1536]{1,0:T(8,128)(2,1)}, u32[]{:S(2)}) copy-start(bf16[512,1536]{1,0:T(8,128)(2,1)} %p3_ref.1) | copy-start | bytes 4718596
  21.0 4.6 %copy-start.3 = (bf16[1024,512]{1,0:T(8,128)(2,1)S(1)}, bf16[1024,512]{1,0:T(8,128)(2,1)}, u32[]{:S(2)}) copy-start(bf16[1024,512]{1,0:T(8,128)(2,1)} %mw2_ref.1) | copy-start | bytes 3145732
  21.0 4.6 %copy-start.4 = (bf16[512,512]{1,0:T(8,128)(2,1)S(1)}, bf16[512,512]{1,0:T(8,128)(2,1)}, u32[]{:S(2)}) copy-start(bf16[512,512]{1,0:T(8,128)(2,1)} %ow3_ref.1) | copy-start | bytes 1572868
  21.0 4.6 %copy-start.10 = (f32[1024]{0:T(1024)S(1)}, f32[1024]{0:T(1024)}, u32[]{:S(2)}) copy-start(f32[1024]{0:T(1024)} %param.26) | copy-start | bytes 12292
  21.0 4.6 %copy-start.11 = (f32[512]{0:T(512)S(1)}, f32[512]{0:T(512)}, u32[]{:S(2)}) copy-start(f32[512]{0:T(512)} %param.28) | copy-start | bytes 6148
  32.5 9.2 %collective-permute-start.5 = (bf16[4,5,28,128]{3,2,1,0:T(8,128)(2,1)S(1)}, bf16[4,5,28,128]{3,2,1,0:T(8,128)(2,1)S(1)}, u32[]{:S(2)}, u32[]{:S(2)}) collective-permute-start(bf16[4,5,28,128]{3,2,1,0:T(8,128)(2,1)S(1)} %get-tuple-element.83), channel_id=1, source_target_pairs={{0,4},{4,8},{8,12},{12,16},{16,20},{20,24},{24,28},{28,0},{1,5},{5... | collective-permute-start | bytes 430088 | tf_op jit(solution)/shard_map/ppermute | solution.py:872
  39.6 9.3 %collective-permute-start.7 = (bf16[15,28,2,128]{3,2,1,0:T(2,128)(2,1)S(1)}, bf16[15,28,2,128]{3,2,1,0:T(2,128)(2,1)S(1)}, u32[]{:S(2)}, u32[]{:S(2)}) collective-permute-start(bf16[15,28,2,128]{3,2,1,0:T(2,128)(2,1)S(1)} %bitcast.56), channel_id=1, source_target_pairs={{0,2},{2,0},{1,3},{3,1},{4,6},{6,4},{5,7},{7,5},{8,10},{10,8},{9,1... | collective-permute-start | bytes 645128 | tf_op jit(solution)/shard_map/ppermute | solution.py:872
  40.4 8.5 %collective-permute-start.8 = (bf16[4,6,28,128]{3,2,1,0:T(8,128)(2,1)S(1)}, bf16[4,6,28,128]{3,2,1,0:T(8,128)(2,1)S(1)}, u32[]{:S(2)}, u32[]{:S(2)}) collective-permute-start(bf16[4,6,28,128]{3,2,1,0:T(8,128)(2,1)S(1)} %get-tuple-element.110), channel_id=1, source_target_pairs={{0,4},{4,8},{8,12},{12,16},{16,20},{20,24},{24,28},{28,0},{1,5},{5... | collective-permute-start | bytes 516104 | tf_op jit(solution)/shard_map/ppermute | solution.py:872
  47.5 6.8 %collective-permute-start.6 = (bf16[14,28,2,128]{3,2,1,0:T(2,128)(2,1)S(1)}, bf16[14,28,2,128]{3,2,1,0:T(2,128)(2,1)S(1)}, u32[]{:S(2)}, u32[]{:S(2)}) collective-permute-start(bf16[14,28,2,128]{3,2,1,0:T(2,128)(2,1)S(1)} %bitcast.58), channel_id=1, source_target_pairs={{0,2},{2,0},{1,3},{3,1},{4,6},{6,4},{5,7},{7,5},{8,10},{10,8},{9,1... | collective-permute-start | bytes 602120 | tf_op jit(solution)/shard_map/ppermute | solution.py:872
  49.0 5.3 %collective-permute-start.9 = (bf16[2,6,28,128]{3,2,1,0:T(8,128)(2,1)S(1)}, bf16[2,6,28,128]{3,2,1,0:T(8,128)(2,1)S(1)}, u32[]{:S(2)}, u32[]{:S(2)}) collective-permute-start(bf16[2,6,28,128]{3,2,1,0:T(8,128)(2,1)S(1)} %slice.3), channel_id=1, source_target_pairs={{0,2},{2,0},{1,3},{3,1},{4,6},{6,4},{5,7},{7,5},{8,10},{10,8},{9,1... | collective-permute-start | bytes 258056 | tf_op jit(solution)/shard_map/ppermute | solution.py:872
  (2 other events, 3.5 us)

commit v3 on v2

--- a/solution.py
+++ b/solution.py
@@ -17,6 +17,7 @@
 SS = 3
 EPSILON = 1e-05
 NREL = 1183
+WIDTH = 28
 LOG2E = 1.4426950408889634
 HEAD = 32
 SCALE = HEAD**-0.5
@@ -146,7 +147,7 @@
     return lax.broadcasted_iota(jnp.int32, shape, 1)
 
 
-def region_rows(ids, section):
+def region_rows(ids, section, place_of):
     columns = ids.shape[1]
     count = columns // WS
     place = lax.broadcasted_iota(jnp.int32, (columns, LANES * count), 0)
@@ -157,17 +158,24 @@
         column = jnp.where(column < 3, column + 4, column - 3)
     chosen = real & (place == lane // LANES * WS + column)
     spread = dot(ids.astype(F32).astype(BF), chosen.astype(F32).astype(BF))
-    row = lax.broadcasted_iota(jnp.int32, spread.shape, 0)
-    lane = lanes_of(spread.shape)
-    real = (lane[:1] % 8 < WS) & (lane[:1] % LANES < ROWS)
+    lane = lanes_of((1, LANES))
+    real = (lane % 8 < WS) & (lane < ROWS)
     rows = []
     for hw in range(ids.shape[0] // (WT * WS)):
-        mine = lane % LANES // 8 == row % 4 * WS + row // 4 - WS * hw
-        inside = (row >= WT * WS * hw) & (row < WT * WS * (hw + 1))
-        found = jnp.sum(jnp.where(mine & inside, spread, 0.0), 0, keepdims=True)
-        found = jnp.where(real, found, -1.0)
-        rows += [found[:, LANES * ww : LANES * (ww + 1)] for ww in range(count)]
+        mine = place_of == float(hw)
+        for ww in range(count):
+            part = jnp.where(mine, spread[:, LANES * ww : LANES * (ww + 1)], 0.0)
+            rows.append(jnp.where(real, jnp.sum(part, 0, keepdims=True), -1.0))
     return rows
+
+
+def id_places():
+    places = np.full((WIDTH * WT, LANES), -1.0, np.float32)
+    for row in range(WIDTH * WT):
+        height, frame = row // WT, row % WT
+        at = (frame * WS + height % WS) * 8
+        places[row, at : at + 8] = height // WS
+    return jnp.asarray(places)
 
 
 def region_columns(ids, section):
@@ -181,13 +189,15 @@
     if section == 3:
         column = jnp.where(column < 3, column + 4, jnp.where(column == 7, 8, column - 3))
     ones = jnp.ones((columns, 128), BF)
+    ahead = lane - column
+    wanted = token // 8 % WS * WT + token // 56
     pad = lax.broadcasted_iota(jnp.int32, (ROWS, 128), 0) % 8 == 7
     found = []
     for hw in range(ids.shape[0] // (WT * WS)):
-        chosen = place == (token // 8 % WS + WS * hw) * WT + token // 56
+        chosen = place - WS * WT * hw == wanted
         picked = dot(chosen.astype(F32).astype(BF), source)
         for ww in range(count):
-            mine = jnp.where(lane == WS * ww + column, picked, 0.0).astype(BF)
+            mine = jnp.where(ahead == WS * ww, picked, 0.0).astype(BF)
             found.append(jnp.where(pad, -1.0, dot(mine, ones)))
     return found
 
@@ -206,7 +216,7 @@
 
 
 def prepare_kernel(
-    t1_ref, t3_ref, s_ref, r1_ref, r3_ref, o1_ref, spread, row1_ref, row3_ref, col1_ref, col3_ref, tab
+    t1_ref, t3_ref, s_ref, r1_ref, r3_ref, place_ref, o1_ref, spread, row1_ref, row3_ref, col1_ref, col3_ref, tab
 ):
     tab[...] = jnp.zeros((24, SPAN), F32)
     tab[0:4, 0:NREL] = t1_ref[...] * LOG2E
@@ -240,9 +250,9 @@
             left, right = bias_rows(spread, 0, HEADS1, tj, hj)
             o1_ref[:, row : row + 8, 0:128] = left
             o1_ref[:, row : row + 8, 128:256] = right
-    for i, found in enumerate(region_rows(r1_ref[...], 1)):
+    for i, found in enumerate(region_rows(r1_ref[...], 1, place_ref[...])):
         row1_ref[i] = found
-    row3_ref[...] = region_rows(r3_ref[...], 3)[0]
+    row3_ref[...] = region_rows(r3_ref[...], 3, place_ref[0 : WT * WS])[0]
     for i, found in enumerate(region_columns(r1_ref[...], 1)):
         col1_ref[i] = found
     col3_ref[...] = region_columns(r3_ref[...], 3)[0]
@@ -281,6 +291,7 @@
         chooser(),
         by_height(regions_one),
         by_height(regions_three),
+        id_places(),
     )
 
 

time: 55.7 us -> 55.8 us (level)
    unnamed x34 -> x36, local copies, waits for them, and re-layouts: 1.46 us -> 1.46 us
where the time goes in v3:
time: 55.8 us; the launch traced here: 55.6 us
  Pallas kernels  31.2 us (56%)
  starting transfers between devices  17.9 us (32%)
  waiting for transfers between devices  2.91 us (5%)
  local copies, waits for them, and re-layouts  2.37 us (4%)
  between operations  1.25 us (2%)
    ppermute x10, starting transfers between devices, send(): return lax.ppermute(values, tuple(axes), pairs)  17.9 us
    pallas_call x2, Pallas kernels, back(): pl.pallas_call(functools.partial(back_kernel, late), out_shape=[jax.Shape...  10.3 us
    pallas_call x2, Pallas kernels, front(): pl.pallas_call(functools.partial(front_kernel, late), out_shape=[jax.Shap...  7.72 us
    pallas_call x1, Pallas kernels, middle(): pl.pallas_call(middle_kernel, out_shape=[jax.ShapeDtypeStruct((576, 256),...  6.92 us
    ppermute x10, waiting for transfers between devices, send(): return lax.ppermute(values, tuple(axes), pairs)  2.91 us
    pallas_call x4, Pallas kernels, merge_call(): pl.pallas_call(kernel, out_shape=[jax.ShapeDtypeStruct(shape, kind) for s...  2.2 us
    pallas_call x1, Pallas kernels, prepare(): pl.pallas_call(prepare_kernel, out_shape=(jax.ShapeDtypeStruct((HEADS1, R...  1.74 us
    unnamed x36, local copies, waits for them, and re-layouts  1.46 us
  transfers between devices with their start and end apart: 10, of which 1 were waited for; matrix products, arithmetic and copies ran while one was open for 1% of the time, Pallas kernels for 42%

profile of v3, /device:TPU:0, one launch (start us, length us, event | category | flops | bytes accessed | tf_op | source)
XLA Modules:
  0.0 55.6 jit_solution(402437566738375222)
XLA Ops:
  0.6 1.3 %copy.39.tok_ref.refs_0_ = bf16[4,28,28,128]{3,2,1,0:T(8,128)(2,1)S(1)} copy(bf16[4,28,28,128]{3,0,2,1:T(4,128)(2,1)} %param.18) | data formatting | bytes 1605632 | tf_op args[0]
  2.1 0.2 copy.65
  2.3 3.0 %collective-permute-start = (bf16[14,28,2,128]{3,2,1,0:T(2,128)(2,1)S(1)}, bf16[14,28,2,128]{3,2,1,0:T(2,128)(2,1)S(1)}, u32[]{:S(2)}, u32[]{:S(2)}) collective-permute-start(bf16[14,28,2,128]{3,2,1,0:T(2,128)(2,1)S(1)} %bitcast.57), channel_id=1, source_target_pairs={{0,2},{2,0},{1,3},{3,1},{4,6},{6,4},{5,7},{7,5},{8,10},{10,8},{9,1... | collective-permute-start | bytes 602120 | tf_op jit(solution)/shard_map/ppermute | solution.py:883
  5.7 5.1 %collective-permute-start.3 = (bf16[2,6,28,128]{3,2,1,0:T(8,128)(2,1)S(1)}, bf16[2,6,28,128]{3,2,1,0:T(8,128)(2,1)S(1)}, u32[]{:S(2)}, u32[]{:S(2)}) collective-permute-start(bf16[2,6,28,128]{3,2,1,0:T(8,128)(2,1)S(1)} %get-tuple-element.73), channel_id=1, source_target_pairs={{0,28},{4,0},{8,4},{12,8},{16,12},{20,16},{24,20},{28,24},{1,29},{... | collective-permute-start | bytes 258056 | tf_op jit(solution)/shard_map/ppermute | solution.py:883
  10.7 1.4 %collective-permute-start.4 = (bf16[2,6,28,128]{3,2,1,0:T(8,128)(2,1)S(1)}, bf16[2,6,28,128]{3,2,1,0:T(8,128)(2,1)S(1)}, u32[]{:S(2)}, u32[]{:S(2)}) collective-permute-start(bf16[2,6,28,128]{3,2,1,0:T(8,128)(2,1)S(1)} %get-tuple-element.74), channel_id=1, source_target_pairs={{0,30},{2,28},{4,2},{6,0},{8,6},{10,4},{12,10},{14,8},{16,14},{18,... | collective-permute-start | bytes 258056 | tf_op jit(solution)/shard_map/ppermute | solution.py:883
  12.3 1.7 %shard_map.186 = (f32[4,224,256]{2,1,0:T(8,128)S(1)}, f32[7,192,128]{2,1,0:T(8,128)S(1)}, f32[16,1,256]{2,1,0:T(1,128)S(1)}, f32[1,256]{1,0:T(1,128)S(1)}, f32[1...) custom-call(f32[4,1183]{1,0:T(4,128)S(1)} %bitcast.48, f32[16,1183]{1,0:T(8,128)S(1)} %bitcast.46, ...), custom_call_target="tpu_custom_call" | custom-call | flops 1650000000 | bytes 1500000 | tf_op jit(solution)/shard_map/pallas_call | solution.py:275
  14.1 3.9 %shard_map.187 = (bf16[4,9,28,128]{3,2,1,0:T(8,128)(2,1)S(1)}, bf16[4,5,28,128]{3,2,1,0:T(8,128)(2,1)S(1)}, f32[16,112,256]{2,1,0:T(8,128)S(1)}, bf16[8,224,128]...) custom-call(bf16[4,28,28,128]{3,2,1,0:T(8,128)(2,1)S(1)} %copy.39.to, ...), custom_call_target="tpu_custom_call" | custom-call | flops 5059999744 | bytes 4600000 | tf_op jit(solution)/shard_map/pallas_call | solution.py:446
  18.0 0.4 shard_map.188
  18.5 2.4 %collective-permute-start.1 = (bf16[4,5,28,128]{3,2,1,0:T(8,128)(2,1)S(1)}, bf16[4,5,28,128]{3,2,1,0:T(8,128)(2,1)S(1)}, u32[]{:S(2)}, u32[]{:S(2)}) collective-permute-start(bf16[4,5,28,128]{3,2,1,0:T(8,128)(2,1)S(1)} %get-tuple-element.68), channel_id=1, source_target_pairs={{0,28},{4,0},{8,4},{12,8},{16,12},{20,16},{24,20},{28,24},{1,29},{... | collective-permute-start | bytes 430088 | tf_op jit(solution)/shard_map/ppermute | solution.py:883
  21.0 3.9 %shard_map.190 = (bf16[4,14,28,128]{3,2,1,0:T(8,128)(2,1)S(1)}, f32[16,112,256]{2,1,0:T(8,128)S(1)}, bf16[8,224,128]{2,1,0:T(8,128)(2,1)S(1)}, bf16[8,224,256]{2...) custom-call(bf16[4,28,28,128]{3,2,1,0:T(8,128)(2,1)S(1)} %copy.39.to, ...), custom_call_target="tpu_custom_call" | custom-call | flops 5059999744 | bytes 4600000 | tf_op jit(solution)/shard_map/pallas_call | solution.py:446
  24.9 0.6 %shard_map.191 = (f32[576,256]{1,0:T(8,128)S(1)}, f32[576,512]{1,0:T(8,128)S(1)}, f32[576,128]{1,0:T(8,128)S(1)}) custom-call(bf16[4,5,28,128]{3,2,1,0:T(8,128)(2,1)S(1)} %get-tuple-element.71.resA_ref, bf16[4,14,28,128]{3,2,1,0:T(8,128)(2,1)S(1)} %get-tuple-element.75.resB_ref, f32[1,512]{1,0:T(1,128)S(1)} %bitcast.42, bf16[512,256]{1,0:T(8,128)(2,1)S(1)} %copy-done), custom_call_target="tpu_custom_call" | custom-call | flops 110000000 | bytes 100000 | tf_op jit(solution)/shard_map/pallas_call | solution.py:630
  25.6 6.9 %shard_map.192 = (f32[576,256]{1,0:T(8,128)S(1)}, bf16[4,28,128]{2,1,0:T(8,128)(2,1)S(1)}, bf16[4,5,28,128]{3,2,1,0:T(8,128)(2,1)S(1)}, bf16[2,4,28,128]{3,2,1,0...) custom-call(f32[576,256]{1,0:T(8,128)S(1)} %get-tuple-element.77.merged_ref, ...), custom_call_target="tpu_custom_call" | custom-call | flops 9900000256 | bytes 9000000 | tf_op jit(solution)/shard_map/pallas_call | solution.py:757
  32.5 1.1 %collective-permute-start.5 = (bf16[4,5,28,128]{3,2,1,0:T(8,128)(2,1)S(1)}, bf16[4,5,28,128]{3,2,1,0:T(8,128)(2,1)S(1)}, u32[]{:S(2)}, u32[]{:S(2)}) collective-permute-start(bf16[4,5,28,128]{3,2,1,0:T(8,128)(2,1)S(1)} %get-tuple-element.83), channel_id=1, source_target_pairs={{0,4},{4,8},{8,12},{12,16},{16,20},{20,24},{24,28},{28,0},{1,5},{5... | collective-permute-start | bytes 430088 | tf_op jit(solution)/shard_map/ppermute | solution.py:883
  33.7 0.7 %shard_map.193 = (bf16[4,5,28,128]{3,2,1,0:T(8,128)(2,1)S(1)}, bf16[4,14,28,128]{3,2,1,0:T(8,128)(2,1)S(1)}) custom-call(f32[576,256]{1,0:T(8,128)S(1)} %get-tuple-element.84.grad_ref, bf16[4,28,128]{2,1,0:T(8,128)(2,1)S(1)} %get-tuple-element.85.d30_ref, f32[576,512]{1,0:T(8,128)S(1)} %get-tuple-element.86.xhat_ref, ...), custom_call_target="tpu_custom_call" | custom-call | flops 1100000000 | bytes 1000000 | tf_op jit(solution)/shard_map/pallas_call | solution.py:630
  34.4 5.2 %shard_map.194 = (bf16[2,11,28,128]{3,2,1,0:T(8,128)(2,1)S(1)}, bf16[2,15,28,128]{3,2,1,0:T(8,128)(2,1)S(1)}, bf16[4,6,28,128]{3,2,1,0:T(8,128)(2,1)S(1)}) custom-call(bf16[4,14,28,128]{3,2,1,0:T(8,128)(2,1)S(1)} %get-tuple-element.88.refs_0_, bf16[2,7,28,128]{3,2,1,0:T(8,128)(2,1)S(1)} %get-tuple-element.89.refs_1_, ...), custom_call_target="tpu_custom_call" | custom-call | flops 6049999872 | bytes 5500000 | tf_op jit(solution)/shard_map/pallas_call | solution.py:524
  39.7 0.7 %collective-permute-start.7 = (bf16[15,28,2,128]{3,2,1,0:T(2,128)(2,1)S(1)}, bf16[15,28,2,128]{3,2,1,0:T(2,128)(2,1)S(1)}, u32[]{:S(2)}, u32[]{:S(2)}) collective-permute-start(bf16[15,28,2,128]{3,2,1,0:T(2,128)(2,1)S(1)} %bitcast.56), channel_id=1, source_target_pairs={{0,2},{2,0},{1,3},{3,1},{4,6},{6,4},{5,7},{7,5},{8,10},{10,8},{9,1... | collective-permute-start | bytes 645128 | tf_op jit(solution)/shard_map/ppermute | solution.py:883
  40.4 1.3 %collective-permute-start.8 = (bf16[4,6,28,128]{3,2,1,0:T(8,128)(2,1)S(1)}, bf16[4,6,28,128]{3,2,1,0:T(8,128)(2,1)S(1)}, u32[]{:S(2)}, u32[]{:S(2)}) collective-permute-start(bf16[4,6,28,128]{3,2,1,0:T(8,128)(2,1)S(1)} %get-tuple-element.110), channel_id=1, source_target_pairs={{0,4},{4,8},{8,12},{12,16},{16,20},{20,24},{24,28},{28,0},{1,5},{5... | collective-permute-start | bytes 516104 | tf_op jit(solution)/shard_map/ppermute | solution.py:883
  41.7 0.4 shard_map.195.refs_0_
  42.1 5.1 %shard_map.196 = (bf16[2,14,28,128]{3,2,1,0:T(8,128)(2,1)S(1)}, bf16[2,14,28,128]{3,2,1,0:T(8,128)(2,1)S(1)}) custom-call(bf16[4,9,28,128]{3,2,1,0:T(8,128)(2,1)S(1)} %shard_map.195.refs_0_, bf16[4,5,28,128]{3,2,1,0:T(8,128)(2,1)S(1)} %get-tuple-element.101.refs_1_, f32[1,128]{1,0:T(1,128)S(1)} %bitcast.54, bf16[128,384]{1,0:T(8,128)(2,1)S(1)} %copy-done.5, ...), custom_call_target="tpu_custom_call" | custom-call | flops 6049999872 | bytes 5500000 | tf_op jit(solution)/shard_map/pallas_call | solution.py:524
  47.5 1.5 %collective-permute-start.6 = (bf16[14,28,2,128]{3,2,1,0:T(2,128)(2,1)S(1)}, bf16[14,28,2,128]{3,2,1,0:T(2,128)(2,1)S(1)}, u32[]{:S(2)}, u32[]{:S(2)}) collective-permute-start(bf16[14,28,2,128]{3,2,1,0:T(2,128)(2,1)S(1)} %bitcast.58), channel_id=1, source_target_pairs={{0,2},{2,0},{1,3},{3,1},{4,6},{6,4},{5,7},{7,5},{8,10},{10,8},{9,1... | collective-permute-start | bytes 602120 | tf_op jit(solution)/shard_map/ppermute | solution.py:883
  49.1 1.2 %collective-permute-start.9 = (bf16[2,6,28,128]{3,2,1,0:T(8,128)(2,1)S(1)}, bf16[2,6,28,128]{3,2,1,0:T(8,128)(2,1)S(1)}, u32[]{:S(2)}, u32[]{:S(2)}) collective-permute-start(bf16[2,6,28,128]{3,2,1,0:T(8,128)(2,1)S(1)} %slice.3), channel_id=1, source_target_pairs={{0,2},{2,0},{1,3},{3,1},{4,6},{6,4},{5,7},{7,5},{8,10},{10,8},{9,1... | collective-permute-start | bytes 258056 | tf_op jit(solution)/shard_map/ppermute | solution.py:883
  50.3 1.2 %shard_map.197 = (bf16[28,28,4,128]{3,2,1,0:T(4,128)(2,1)}, bf16[7,7,4,512]{3,2,1,0:T(4,128)(2,1)}) custom-call(bf16[2,15,28,128]{3,2,1,0:T(8,128)(2,1)S(1)} %bitcast.38, bf16[2,11,28,128]{3,2,1,0:T(8,128)(2,1)S(1)} %get-tuple-element.114.own_ref, bf16[2,4,28,128]{3,2,1,0:T(8,128)(2,1)S(1)} %get-tuple-element.115.so_ref), custom_call_target="tpu_custom_call" | custom-call | flops 2200000000 | bytes 2000000 | tf_op jit(solution)/shard_map/pallas_call | solution.py:803
  51.5 2.9 %collective-permute-done.9.dg_ref = bf16[2,6,28,128]{3,2,1,0:T(8,128)(2,1)S(1)} collective-permute-done((bf16[2,6,28,128]{3,2,1,0:T(8,128)(2,1)S(1)}, bf16[2,6,28,128]{3,2,1,0:T(8,128)(2,1)S(1)}, u32[]{:S(2)}, u32[]{:S(2)}) %collective-permute-start.9) | collective-permute-done | bytes 86048 | tf_op jit(solution)/shard_map/ppermute | solution.py:883
  54.4 1.1 %shard_map.198 = (bf16[28,28,4,128]{3,2,1,0:T(4,128)(2,1)}, bf16[7,7,4,512]{3,2,1,0:T(4,128)(2,1)}) custom-call(bf16[28,28,4,128]{3,2,1,0:T(4,128)(2,1)} %get-tuple-element.117.grad_hbm, bf16[7,7,4,512]{3,2,1,0:T(4,128)(2,1)} %get-tuple-element.118.section_hbm, bf16[2,14,28,128]{3,2,1,0:T(8,128)(2,1)S(1)} %bitcast.40, ...), custom_call_target="tpu_custom_call", output_to_operand_aliasing={{0}: (0, {}), {1}: (1, {})} | custom-call | flops 1100000000 | bytes 1000000 | tf_op jit(solution)/shard_map/pallas_call | solution.py:843
  (56 shorter events, 1.0 us)
Async XLA Ops:
  0.6 4.7 %copy-start.15 = (bf16[4,7,7,512]{3,0,2,1:T(4,128)(2,1)S(1)}, bf16[4,7,7,512]{3,0,2,1:T(4,128)(2,1)}, u32[]{:S(2)}) copy-start(bf16[4,7,7,512]{3,0,2,1:T(4,128)(2,1)} %param.33) | copy-start | bytes 602116
  2.0 10.2 %copy-start.16 = (s32[4,7,7]{2,0,1:T(4,128)S(1)}, s32[4,7,7]{2,0,1:T(4,128)}, u32[]{:S(2)}) copy-start(s32[4,7,7]{2,0,1:T(4,128)} %param.20) | copy-start | bytes 2356
  2.0 10.2 %copy-start.6 = (f32[1183,16]{0,1:T(8,128)S(1)}, f32[1183,16]{0,1:T(8,128)}, u32[]{:S(2)}) copy-start(f32[1183,16]{0,1:T(8,128)} %param.32) | copy-start | bytes 227140
  2.0 10.2 %copy-start.7 = (s32[4,28,28]{2,0,1:T(4,128)S(1)}, s32[4,28,28]{2,0,1:T(4,128)}, u32[]{:S(2)}) copy-start(s32[4,28,28]{2,0,1:T(4,128)} %param.19) | copy-start | bytes 37636
  2.0 10.2 %copy-start.9 = (f32[1183,4]{0,1:T(4,128)S(1)}, f32[1183,4]{0,1:T(4,128)}, u32[]{:S(2)}) copy-start(f32[1183,4]{0,1:T(4,128)} %param.24) | copy-start | bytes 56788
  2.0 10.2 %copy-start.13 = (bf16[256,1024]{1,0:T(8,128)(2,1)S(1)}, bf16[256,1024]{1,0:T(8,128)(2,1)}, u32[]{:S(2)}) copy-start(bf16[256,1024]{1,0:T(8,128)(2,1)} %constant.4.clone.s_ref) | copy-start | bytes 1572868
  2.0 10.2 %copy-start.14 = (f32[112,256]{1,0:T(8,128)S(1)}, f32[112,256]{1,0:T(8,128)}, u32[]{:S(2)}) copy-start(f32[112,256]{1,0:T(8,128)} %constant.5.clone.place_ref) | copy-start | bytes 344068
  2.3 11.7 %collective-permute-start = (bf16[14,28,2,128]{3,2,1,0:T(2,128)(2,1)S(1)}, bf16[14,28,2,128]{3,2,1,0:T(2,128)(2,1)S(1)}, u32[]{:S(2)}, u32[]{:S(2)}) collective-permute-start(bf16[14,28,2,128]{3,2,1,0:T(2,128)(2,1)S(1)} %bitcast.57), channel_id=1, source_target_pairs={{0,2},{2,0},{1,3},{3,1},{4,6},{6,4},{5,7},{7,5},{8,10},{10,8},{9,1... | collective-permute-start | bytes 602120 | tf_op jit(solution)/shard_map/ppermute | solution.py:883
  5.6 15.3 %collective-permute-start.2 = (bf16[15,28,2,128]{3,2,1,0:T(2,128)(2,1)S(1)}, bf16[15,28,2,128]{3,2,1,0:T(2,128)(2,1)S(1)}, u32[]{:S(2)}, u32[]{:S(2)}) collective-permute-start(bf16[15,28,2,128]{3,2,1,0:T(2,128)(2,1)S(1)} %bitcast.55), channel_id=1, source_target_pairs={{0,2},{2,0},{1,3},{3,1},{4,6},{6,4},{5,7},{7,5},{8,10},{10,8},{9,1... | collective-permute-start | bytes 645128 | tf_op jit(solution)/shard_map/ppermute | solution.py:883
  5.7 15.3 %collective-permute-start.3 = (bf16[2,6,28,128]{3,2,1,0:T(8,128)(2,1)S(1)}, bf16[2,6,28,128]{3,2,1,0:T(8,128)(2,1)S(1)}, u32[]{:S(2)}, u32[]{:S(2)}) collective-permute-start(bf16[2,6,28,128]{3,2,1,0:T(8,128)(2,1)S(1)} %get-tuple-element.73), channel_id=1, source_target_pairs={{0,28},{4,0},{8,4},{12,8},{16,12},{20,16},{24,20},{28,24},{1,29},{... | collective-permute-start | bytes 258056 | tf_op jit(solution)/shard_map/ppermute | solution.py:883
  10.7 10.2 %collective-permute-start.4 = (bf16[2,6,28,128]{3,2,1,0:T(8,128)(2,1)S(1)}, bf16[2,6,28,128]{3,2,1,0:T(8,128)(2,1)S(1)}, u32[]{:S(2)}, u32[]{:S(2)}) collective-permute-start(bf16[2,6,28,128]{3,2,1,0:T(8,128)(2,1)S(1)} %get-tuple-element.74), channel_id=1, source_target_pairs={{0,30},{2,28},{4,2},{6,0},{8,6},{10,4},{12,10},{14,8},{16,14},{18,... | collective-permute-start | bytes 258056 | tf_op jit(solution)/shard_map/ppermute | solution.py:883
  14.1 3.9 %copy-start = (bf16[512,256]{1,0:T(8,128)(2,1)S(1)}, bf16[512,256]{1,0:T(8,128)(2,1)}, u32[]{:S(2)}) copy-start(bf16[512,256]{1,0:T(8,128)(2,1)} %weight_ref.7) | copy-start | bytes 786436
  14.1 3.9 %copy-start.1 = (f32[512]{0:T(512)S(1)}, f32[512]{0:T(512)}, u32[]{:S(2)}) copy-start(f32[512]{0:T(512)} %param.25) | copy-start | bytes 6148
  18.5 7.1 %collective-permute-start.1 = (bf16[4,5,28,128]{3,2,1,0:T(8,128)(2,1)S(1)}, bf16[4,5,28,128]{3,2,1,0:T(8,128)(2,1)S(1)}, u32[]{:S(2)}, u32[]{:S(2)}) collective-permute-start(bf16[4,5,28,128]{3,2,1,0:T(8,128)(2,1)S(1)} %get-tuple-element.68), channel_id=1, source_target_pairs={{0,28},{4,0},{8,4},{12,8},{16,12},{20,16},{24,20},{28,24},{1,29},{... | collective-permute-start | bytes 430088 | tf_op jit(solution)/shard_map/ppermute | solution.py:883
  21.0 4.6 %copy-start.2 = (bf16[512,1536]{1,0:T(8,128)(2,1)S(1)}, bf16[512,1536]{1,0:T(8,128)(2,1)}, u32[]{:S(2)}) copy-start(bf16[512,1536]{1,0:T(8,128)(2,1)} %p3_ref.1) | copy-start | bytes 4718596
  21.0 4.6 %copy-start.3 = (bf16[1024,512]{1,0:T(8,128)(2,1)S(1)}, bf16[1024,512]{1,0:T(8,128)(2,1)}, u32[]{:S(2)}) copy-start(bf16[1024,512]{1,0:T(8,128)(2,1)} %mw2_ref.1) | copy-start | bytes 3145732
  21.0 4.6 %copy-start.4 = (bf16[512,512]{1,0:T(8,128)(2,1)S(1)}, bf16[512,512]{1,0:T(8,128)(2,1)}, u32[]{:S(2)}) copy-start(bf16[512,512]{1,0:T(8,128)(2,1)} %ow3_ref.1) | copy-start | bytes 1572868
  21.0 4.6 %copy-start.10 = (f32[1024]{0:T(1024)S(1)}, f32[1024]{0:T(1024)}, u32[]{:S(2)}) copy-start(f32[1024]{0:T(1024)} %param.27) | copy-start | bytes 12292
  21.0 4.6 %copy-start.11 = (f32[512]{0:T(512)S(1)}, f32[512]{0:T(512)}, u32[]{:S(2)}) copy-start(f32[512]{0:T(512)} %param.29) | copy-start | bytes 6148
  32.5 9.2 %collective-permute-start.5 = (bf16[4,5,28,128]{3,2,1,0:T(8,128)(2,1)S(1)}, bf16[4,5,28,128]{3,2,1,0:T(8,128)(2,1)S(1)}, u32[]{:S(2)}, u32[]{:S(2)}) collective-permute-start(bf16[4,5,28,128]{3,2,1,0:T(8,128)(2,1)S(1)} %get-tuple-element.83), channel_id=1, source_target_pairs={{0,4},{4,8},{8,12},{12,16},{16,20},{20,24},{24,28},{28,0},{1,5},{5... | collective-permute-start | bytes 430088 | tf_op jit(solution)/shard_map/ppermute | solution.py:883
  39.7 9.3 %collective-permute-start.7 = (bf16[15,28,2,128]{3,2,1,0:T(2,128)(2,1)S(1)}, bf16[15,28,2,128]{3,2,1,0:T(2,128)(2,1)S(1)}, u32[]{:S(2)}, u32[]{:S(2)}) collective-permute-start(bf16[15,28,2,128]{3,2,1,0:T(2,128)(2,1)S(1)} %bitcast.56), channel_id=1, source_target_pairs={{0,2},{2,0},{1,3},{3,1},{4,6},{6,4},{5,7},{7,5},{8,10},{10,8},{9,1... | collective-permute-start | bytes 645128 | tf_op jit(solution)/shard_map/ppermute | solution.py:883
  40.4 8.6 %collective-permute-start.8 = (bf16[4,6,28,128]{3,2,1,0:T(8,128)(2,1)S(1)}, bf16[4,6,28,128]{3,2,1,0:T(8,128)(2,1)S(1)}, u32[]{:S(2)}, u32[]{:S(2)}) collective-permute-start(bf16[4,6,28,128]{3,2,1,0:T(8,128)(2,1)S(1)} %get-tuple-element.110), channel_id=1, source_target_pairs={{0,4},{4,8},{8,12},{12,16},{16,20},{20,24},{24,28},{28,0},{1,5},{5... | collective-permute-start | bytes 516104 | tf_op jit(solution)/shard_map/ppermute | solution.py:883
  47.5 6.8 %collective-permute-start.6 = (bf16[14,28,2,128]{3,2,1,0:T(2,128)(2,1)S(1)}, bf16[14,28,2,128]{3,2,1,0:T(2,128)(2,1)S(1)}, u32[]{:S(2)}, u32[]{:S(2)}) collective-permute-start(bf16[14,28,2,128]{3,2,1,0:T(2,128)(2,1)S(1)} %bitcast.58), channel_id=1, source_target_pairs={{0,2},{2,0},{1,3},{3,1},{4,6},{6,4},{5,7},{7,5},{8,10},{10,8},{9,1... | collective-permute-start | bytes 602120 | tf_op jit(solution)/shard_map/ppermute | solution.py:883
  49.1 5.2 %collective-permute-start.9 = (bf16[2,6,28,128]{3,2,1,0:T(8,128)(2,1)S(1)}, bf16[2,6,28,128]{3,2,1,0:T(8,128)(2,1)S(1)}, u32[]{:S(2)}, u32[]{:S(2)}) collective-permute-start(bf16[2,6,28,128]{3,2,1,0:T(8,128)(2,1)S(1)} %slice.3), channel_id=1, source_target_pairs={{0,2},{2,0},{1,3},{3,1},{4,6},{6,4},{5,7},{7,5},{8,10},{10,8},{9,1... | collective-permute-start | bytes 258056 | tf_op jit(solution)/shard_map/ppermute | solution.py:883
  (3 other events, 5.5 us)

commit v4 on v2

--- a/solution.py
+++ b/solution.py
@@ -266,7 +266,7 @@
         prepare_kernel,
         out_shape=(
             jax.ShapeDtypeStruct((HEADS1, ROWS, LANES), F32),
-            jax.ShapeDtypeStruct((7, 24 * 8, 128), F32),
+            jax.ShapeDtypeStruct((7, 25 * 8, 128), F32),
             jax.ShapeDtypeStruct((16, 1, LANES), F32),
             jax.ShapeDtypeStruct((1, LANES), F32),
             jax.ShapeDtypeStruct((16, ROWS, 128), F32),
@@ -619,7 +619,7 @@
     return pl.pallas_call(
         kernel,
         out_shape=[jax.ShapeDtypeStruct(shape, kind) for shape, kind in shapes],
-        scratch_shapes=[pltpu.VMEM((WT, pairs, 2, 32, 128), F32)],
+        scratch_shapes=[pltpu.VMEM((WT, pairs, 2, 40, 128), F32)],
         compiler_params=params(),
         cost_estimate=cost(us),
     )(*operands)
@@ -641,13 +641,13 @@
         for half in range(2):
             block = values[:, 128 * half : 128 * half + 128].reshape(WT, count, 16, 128)
             for i in range(count):
-                stage2[half, :, (first + i) // 2, (first + i) % 2] = block[:, i]
+                stage2[half, :, (first + i) // 2, (first + i) % 2, 0:16] = block[:, i]
 
     def take_merged(first, count):
         halves = [
             jnp.concatenate(
                 [
-                    stage2[half, :, (first + i) // 2, (first + i) % 2].reshape(WT, 1, 16, 128)
+                    stage2[half, :, (first + i) // 2, (first + i) % 2, 0:16].reshape(WT, 1, 16, 128)
                     for i in range(count)
                 ],
                 1,
@@ -748,8 +748,8 @@
         out_shape=[jax.ShapeDtypeStruct((576, 256), F32)]
         + [jax.ShapeDtypeStruct(s, BF) for s in shapes],
         scratch_shapes=[
-            pltpu.VMEM((4, 1, 2, 32, 128), F32),
-            pltpu.VMEM((2, 4, 7, 2, 16, 128), F32),
+            pltpu.VMEM((4, 1, 2, 40, 128), F32),
+            pltpu.VMEM((2, 4, 7, 2, 24, 128), F32),
             pltpu.VMEM((ROWS, 1024), F32),
             pltpu.VMEM((ROWS, 128), F32),
             pltpu.VMEM((4, 7, 8, 512), F32),
@@ -776,9 +776,9 @@
         for g in range(4):
             narrow[g, :, pl.ds(t, 7, stride=4), :] = low[:, 7 * g : 7 * g + 7]
     for i in range(11):
-        grad_ref[17 + i] = wide[i].reshape(28, 4, 128).astype(BF)
+        grad_ref[17 + i] = wide[i, 0:112].reshape(28, 4, 128).astype(BF)
     for i in range(4):
-        row = jnp.concatenate([narrow[g, i] for g in range(4)], 1)
+        row = jnp.concatenate([narrow[g, i, 0:28] for g in range(4)], 1)
         section_ref[3 + i] = row.reshape(7, 4, 512).astype(BF)
 
 
@@ -792,7 +792,7 @@
     return pl.pallas_call(
         join_kernel,
         out_shape=JOINED,
-        scratch_shapes=[pltpu.VMEM((11, 112, 128), F32), pltpu.VMEM((4, 4, 28, 128), F32)],
+        scratch_shapes=[pltpu.VMEM((11, 120, 128), F32), pltpu.VMEM((4, 4, 32, 128), F32)],
         compiler_params=params(),
         cost_estimate=cost(2),
     )(ta, own, section_own)
@@ -811,15 +811,15 @@
         for g in range(4):
             narrow[g, :, pl.ds(t, 7, stride=4), :] = high[:, 7 * g : 7 * g + 7]
     for i in range(8):
-        rows[i] = wide[i].reshape(28, 4, 128).astype(BF)
+        rows[i] = wide[i, 0:112].reshape(28, 4, 128).astype(BF)
     start = pltpu.make_async_copy(rows.at[0:8], grad_out.at[0:8], sems.at[2])
     start.start()
     for i in range(8, 17):
-        rows[i] = wide[i].reshape(28, 4, 128).astype(BF)
+        rows[i] = wide[i, 0:112].reshape(28, 4, 128).astype(BF)
     copy = pltpu.make_async_copy(rows.at[8:17], grad_out.at[8:17], sems.at[0])
     copy.start()
     for i in range(3):
-        row = jnp.concatenate([narrow[g, i] for g in range(4)], 1)
+        row = jnp.concatenate([narrow[g, i, 0:28] for g in range(4)], 1)
         section_rows[i] = row.reshape(7, 4, 512).astype(BF)
     other = pltpu.make_async_copy(section_rows, section_out.at[0:3], sems.at[1])
     other.start()
@@ -836,8 +836,8 @@
         out_specs=[pl.BlockSpec(memory_space=pl.ANY)] * 2,
         out_shape=JOINED,
         scratch_shapes=[
-            pltpu.VMEM((17, 112, 128), F32),
-            pltpu.VMEM((4, 3, 28, 128), F32),
+            pltpu.VMEM((17, 120, 128), F32),
+            pltpu.VMEM((4, 3, 32, 128), F32),
             pltpu.VMEM((17, 28, 4, 128), BF),
             pltpu.VMEM((3, 7, 4, 512), BF),
             pltpu.SemaphoreType.DMA((3,)),

time: 55.7 us -> 55.7 us (level)
  no operation moved by 1% of the time
where the time goes in v4:
time: 55.7 us; the launch traced here: 55.6 us
  Pallas kernels  31.1 us (56%)
  starting transfers between devices  17.9 us (32%)
  waiting for transfers between devices  2.96 us (5%)
  local copies, waits for them, and re-layouts  2.36 us (4%)
  between operations  1.24 us (2%)
    ppermute x10, starting transfers between devices, send(): return lax.ppermute(values, tuple(axes), pairs)  17.9 us
    pallas_call x2, Pallas kernels, back(): pl.pallas_call(functools.partial(back_kernel, late), out_shape=[jax.Shape...  10.3 us
    pallas_call x2, Pallas kernels, front(): pl.pallas_call(functools.partial(front_kernel, late), out_shape=[jax.Shap...  7.74 us
    pallas_call x1, Pallas kernels, middle(): pl.pallas_call(middle_kernel, out_shape=[jax.ShapeDtypeStruct((576, 256),...  6.93 us
    ppermute x10, waiting for transfers between devices, send(): return lax.ppermute(values, tuple(axes), pairs)  2.96 us
    pallas_call x4, Pallas kernels, merge_call(): pl.pallas_call(kernel, out_shape=[jax.ShapeDtypeStruct(shape, kind) for s...  2.17 us
    pallas_call x1, Pallas kernels, prepare(): pl.pallas_call(prepare_kernel, out_shape=(jax.ShapeDtypeStruct((HEADS1, R...  1.68 us
    unnamed x34, local copies, waits for them, and re-layouts  1.46 us
  transfers between devices with their start and end apart: 10, of which 1 were waited for; matrix products, arithmetic and copies ran while one was open for 1% of the time, Pallas kernels for 42%

profile of v4, /device:TPU:0, one launch (start us, length us, event | category | flops | bytes accessed | tf_op | source)
XLA Modules:
  0.0 55.6 jit_solution(2141475442691375615)
XLA Ops:
  0.6 1.3 %copy.38.tok_ref.refs_0_ = bf16[4,28,28,128]{3,2,1,0:T(8,128)(2,1)S(1)} copy(bf16[4,28,28,128]{3,0,2,1:T(4,128)(2,1)} %param.17) | data formatting | bytes 1605632 | tf_op args[0]
  2.1 0.2 copy.64
  2.3 3.0 %collective-permute-start = (bf16[14,28,2,128]{3,2,1,0:T(2,128)(2,1)S(1)}, bf16[14,28,2,128]{3,2,1,0:T(2,128)(2,1)S(1)}, u32[]{:S(2)}, u32[]{:S(2)}) collective-permute-start(bf16[14,28,2,128]{3,2,1,0:T(2,128)(2,1)S(1)} %bitcast.57), channel_id=1, source_target_pairs={{0,2},{2,0},{1,3},{3,1},{4,6},{6,4},{5,7},{7,5},{8,10},{10,8},{9,1... | collective-permute-start | bytes 602120 | tf_op jit(solution)/shard_map/ppermute | solution.py:872
  5.7 5.1 %collective-permute-start.3 = (bf16[2,6,28,128]{3,2,1,0:T(8,128)(2,1)S(1)}, bf16[2,6,28,128]{3,2,1,0:T(8,128)(2,1)S(1)}, u32[]{:S(2)}, u32[]{:S(2)}) collective-permute-start(bf16[2,6,28,128]{3,2,1,0:T(8,128)(2,1)S(1)} %get-tuple-element.73), channel_id=1, source_target_pairs={{0,28},{4,0},{8,4},{12,8},{16,12},{20,16},{24,20},{28,24},{1,29},{... | collective-permute-start | bytes 258056 | tf_op jit(solution)/shard_map/ppermute | solution.py:872
  10.7 1.4 %collective-permute-start.4 = (bf16[2,6,28,128]{3,2,1,0:T(8,128)(2,1)S(1)}, bf16[2,6,28,128]{3,2,1,0:T(8,128)(2,1)S(1)}, u32[]{:S(2)}, u32[]{:S(2)}) collective-permute-start(bf16[2,6,28,128]{3,2,1,0:T(8,128)(2,1)S(1)} %get-tuple-element.74), channel_id=1, source_target_pairs={{0,30},{2,28},{4,2},{6,0},{8,6},{10,4},{12,10},{14,8},{16,14},{18,... | collective-permute-start | bytes 258056 | tf_op jit(solution)/shard_map/ppermute | solution.py:872
  12.3 1.7 %shard_map.177 = (f32[4,224,256]{2,1,0:T(8,128)S(1)}, f32[7,200,128]{2,1,0:T(8,128)S(1)}, f32[16,1,256]{2,1,0:T(1,128)S(1)}, f32[1,256]{1,0:T(1,128)S(1)}, f32[1...) custom-call(f32[4,1183]{1,0:T(4,128)S(1)} %bitcast.48, f32[16,1183]{1,0:T(8,128)S(1)} %bitcast.46, ...), custom_call_target="tpu_custom_call" | custom-call | flops 1650000000 | bytes 1500000 | tf_op jit(solution)/shard_map/pallas_call | solution.py:265
  14.0 3.9 %shard_map.178 = (bf16[4,9,28,128]{3,2,1,0:T(8,128)(2,1)S(1)}, bf16[4,5,28,128]{3,2,1,0:T(8,128)(2,1)S(1)}, f32[16,112,256]{2,1,0:T(8,128)S(1)}, bf16[8,224,128]...) custom-call(bf16[4,28,28,128]{3,2,1,0:T(8,128)(2,1)S(1)} %copy.38.to, ...), custom_call_target="tpu_custom_call" | custom-call | flops 5059999744 | bytes 4600000 | tf_op jit(solution)/shard_map/pallas_call | solution.py:435
  17.9 0.4 shard_map.179
  18.4 2.5 %collective-permute-start.1 = (bf16[4,5,28,128]{3,2,1,0:T(8,128)(2,1)S(1)}, bf16[4,5,28,128]{3,2,1,0:T(8,128)(2,1)S(1)}, u32[]{:S(2)}, u32[]{:S(2)}) collective-permute-start(bf16[4,5,28,128]{3,2,1,0:T(8,128)(2,1)S(1)} %get-tuple-element.68), channel_id=1, source_target_pairs={{0,28},{4,0},{8,4},{12,8},{16,12},{20,16},{24,20},{28,24},{1,29},{... | collective-permute-start | bytes 430088 | tf_op jit(solution)/shard_map/ppermute | solution.py:872
  21.0 3.9 %shard_map.181 = (bf16[4,14,28,128]{3,2,1,0:T(8,128)(2,1)S(1)}, f32[16,112,256]{2,1,0:T(8,128)S(1)}, bf16[8,224,128]{2,1,0:T(8,128)(2,1)S(1)}, bf16[8,224,256]{2...) custom-call(bf16[4,28,28,128]{3,2,1,0:T(8,128)(2,1)S(1)} %copy.38.to, ...), custom_call_target="tpu_custom_call" | custom-call | flops 5059999744 | bytes 4600000 | tf_op jit(solution)/shard_map/pallas_call | solution.py:435
  24.9 0.6 %shard_map.182 = (f32[576,256]{1,0:T(8,128)S(1)}, f32[576,512]{1,0:T(8,128)S(1)}, f32[576,128]{1,0:T(8,128)S(1)}) custom-call(bf16[4,5,28,128]{3,2,1,0:T(8,128)(2,1)S(1)} %get-tuple-element.71.resA_ref, bf16[4,14,28,128]{3,2,1,0:T(8,128)(2,1)S(1)} %get-tuple-element.75.resB_ref, f32[1,512]{1,0:T(1,128)S(1)} %bitcast.42, bf16[512,256]{1,0:T(8,128)(2,1)S(1)} %copy-done), custom_call_target="tpu_custom_call" | custom-call | flops 110000000 | bytes 100000 | tf_op jit(solution)/shard_map/pallas_call | solution.py:619
  25.6 6.9 %shard_map.183 = (f32[576,256]{1,0:T(8,128)S(1)}, bf16[4,28,128]{2,1,0:T(8,128)(2,1)S(1)}, bf16[4,5,28,128]{3,2,1,0:T(8,128)(2,1)S(1)}, bf16[2,4,28,128]{3,2,1,0...) custom-call(f32[576,256]{1,0:T(8,128)S(1)} %get-tuple-element.77.merged_ref, ...), custom_call_target="tpu_custom_call" | custom-call | flops 9900000256 | bytes 9000000 | tf_op jit(solution)/shard_map/pallas_call | solution.py:746
  32.5 1.1 %collective-permute-start.5 = (bf16[4,5,28,128]{3,2,1,0:T(8,128)(2,1)S(1)}, bf16[4,5,28,128]{3,2,1,0:T(8,128)(2,1)S(1)}, u32[]{:S(2)}, u32[]{:S(2)}) collective-permute-start(bf16[4,5,28,128]{3,2,1,0:T(8,128)(2,1)S(1)} %get-tuple-element.83), channel_id=1, source_target_pairs={{0,4},{4,8},{8,12},{12,16},{16,20},{20,24},{24,28},{28,0},{1,5},{5... | collective-permute-start | bytes 430088 | tf_op jit(solution)/shard_map/ppermute | solution.py:872
  33.6 0.7 %shard_map.184 = (bf16[4,5,28,128]{3,2,1,0:T(8,128)(2,1)S(1)}, bf16[4,14,28,128]{3,2,1,0:T(8,128)(2,1)S(1)}) custom-call(f32[576,256]{1,0:T(8,128)S(1)} %get-tuple-element.84.grad_ref, bf16[4,28,128]{2,1,0:T(8,128)(2,1)S(1)} %get-tuple-element.85.d30_ref, f32[576,512]{1,0:T(8,128)S(1)} %get-tuple-element.86.xhat_ref, ...), custom_call_target="tpu_custom_call" | custom-call | flops 1100000000 | bytes 1000000 | tf_op jit(solution)/shard_map/pallas_call | solution.py:619
  34.3 5.2 %shard_map.185 = (bf16[2,11,28,128]{3,2,1,0:T(8,128)(2,1)S(1)}, bf16[2,15,28,128]{3,2,1,0:T(8,128)(2,1)S(1)}, bf16[4,6,28,128]{3,2,1,0:T(8,128)(2,1)S(1)}) custom-call(bf16[4,14,28,128]{3,2,1,0:T(8,128)(2,1)S(1)} %get-tuple-element.88.refs_0_, bf16[2,7,28,128]{3,2,1,0:T(8,128)(2,1)S(1)} %get-tuple-element.89.refs_1_, ...), custom_call_target="tpu_custom_call" | custom-call | flops 6049999872 | bytes 5500000 | tf_op jit(solution)/shard_map/pallas_call | solution.py:513
  39.6 0.8 %collective-permute-start.7 = (bf16[15,28,2,128]{3,2,1,0:T(2,128)(2,1)S(1)}, bf16[15,28,2,128]{3,2,1,0:T(2,128)(2,1)S(1)}, u32[]{:S(2)}, u32[]{:S(2)}) collective-permute-start(bf16[15,28,2,128]{3,2,1,0:T(2,128)(2,1)S(1)} %bitcast.56), channel_id=1, source_target_pairs={{0,2},{2,0},{1,3},{3,1},{4,6},{6,4},{5,7},{7,5},{8,10},{10,8},{9,1... | collective-permute-start | bytes 645128 | tf_op jit(solution)/shard_map/ppermute | solution.py:872
  40.4 1.2 %collective-permute-start.8 = (bf16[4,6,28,128]{3,2,1,0:T(8,128)(2,1)S(1)}, bf16[4,6,28,128]{3,2,1,0:T(8,128)(2,1)S(1)}, u32[]{:S(2)}, u32[]{:S(2)}) collective-permute-start(bf16[4,6,28,128]{3,2,1,0:T(8,128)(2,1)S(1)} %get-tuple-element.110), channel_id=1, source_target_pairs={{0,4},{4,8},{8,12},{12,16},{16,20},{20,24},{24,28},{28,0},{1,5},{5... | collective-permute-start | bytes 516104 | tf_op jit(solution)/shard_map/ppermute | solution.py:872
  41.7 0.4 shard_map.186.refs_0_
  42.1 5.1 %shard_map.187 = (bf16[2,14,28,128]{3,2,1,0:T(8,128)(2,1)S(1)}, bf16[2,14,28,128]{3,2,1,0:T(8,128)(2,1)S(1)}) custom-call(bf16[4,9,28,128]{3,2,1,0:T(8,128)(2,1)S(1)} %shard_map.186.refs_0_, bf16[4,5,28,128]{3,2,1,0:T(8,128)(2,1)S(1)} %get-tuple-element.101.refs_1_, f32[1,128]{1,0:T(1,128)S(1)} %bitcast.54, bf16[128,384]{1,0:T(8,128)(2,1)S(1)} %copy-done.5, ...), custom_call_target="tpu_custom_call" | custom-call | flops 6049999872 | bytes 5500000 | tf_op jit(solution)/shard_map/pallas_call | solution.py:513
  47.5 1.5 %collective-permute-start.6 = (bf16[14,28,2,128]{3,2,1,0:T(2,128)(2,1)S(1)}, bf16[14,28,2,128]{3,2,1,0:T(2,128)(2,1)S(1)}, u32[]{:S(2)}, u32[]{:S(2)}) collective-permute-start(bf16[14,28,2,128]{3,2,1,0:T(2,128)(2,1)S(1)} %bitcast.58), channel_id=1, source_target_pairs={{0,2},{2,0},{1,3},{3,1},{4,6},{6,4},{5,7},{7,5},{8,10},{10,8},{9,1... | collective-permute-start | bytes 602120 | tf_op jit(solution)/shard_map/ppermute | solution.py:872
  49.0 1.2 %collective-permute-start.9 = (bf16[2,6,28,128]{3,2,1,0:T(8,128)(2,1)S(1)}, bf16[2,6,28,128]{3,2,1,0:T(8,128)(2,1)S(1)}, u32[]{:S(2)}, u32[]{:S(2)}) collective-permute-start(bf16[2,6,28,128]{3,2,1,0:T(8,128)(2,1)S(1)} %slice.3), channel_id=1, source_target_pairs={{0,2},{2,0},{1,3},{3,1},{4,6},{6,4},{5,7},{7,5},{8,10},{10,8},{9,1... | collective-permute-start | bytes 258056 | tf_op jit(solution)/shard_map/ppermute | solution.py:872
  50.2 1.2 %shard_map.188 = (bf16[28,28,4,128]{3,2,1,0:T(4,128)(2,1)}, bf16[7,7,4,512]{3,2,1,0:T(4,128)(2,1)}) custom-call(bf16[2,15,28,128]{3,2,1,0:T(8,128)(2,1)S(1)} %bitcast.38, bf16[2,11,28,128]{3,2,1,0:T(8,128)(2,1)S(1)} %get-tuple-element.114.own_ref, bf16[2,4,28,128]{3,2,1,0:T(8,128)(2,1)S(1)} %get-tuple-element.115.so_ref), custom_call_target="tpu_custom_call" | custom-call | flops 2200000000 | bytes 2000000 | tf_op jit(solution)/shard_map/pallas_call | solution.py:792
  51.4 2.9 %collective-permute-done.9.dg_ref = bf16[2,6,28,128]{3,2,1,0:T(8,128)(2,1)S(1)} collective-permute-done((bf16[2,6,28,128]{3,2,1,0:T(8,128)(2,1)S(1)}, bf16[2,6,28,128]{3,2,1,0:T(8,128)(2,1)S(1)}, u32[]{:S(2)}, u32[]{:S(2)}) %collective-permute-start.9) | collective-permute-done | bytes 86048 | tf_op jit(solution)/shard_map/ppermute | solution.py:872
  54.3 1.1 %shard_map.189 = (bf16[28,28,4,128]{3,2,1,0:T(4,128)(2,1)}, bf16[7,7,4,512]{3,2,1,0:T(4,128)(2,1)}) custom-call(bf16[28,28,4,128]{3,2,1,0:T(4,128)(2,1)} %get-tuple-element.117.grad_hbm, bf16[7,7,4,512]{3,2,1,0:T(4,128)(2,1)} %get-tuple-element.118.section_hbm, bf16[2,14,28,128]{3,2,1,0:T(8,128)(2,1)S(1)} %bitcast.40, ...), custom_call_target="tpu_custom_call", output_to_operand_aliasing={{0}: (0, {}), {1}: (1, {})} | custom-call | flops 1100000000 | bytes 1000000 | tf_op jit(solution)/shard_map/pallas_call | solution.py:832
  (54 shorter events, 1.0 us)
Async XLA Ops:
  0.6 4.7 %copy-start.14 = (bf16[4,7,7,512]{3,0,2,1:T(4,128)(2,1)S(1)}, bf16[4,7,7,512]{3,0,2,1:T(4,128)(2,1)}, u32[]{:S(2)}) copy-start(bf16[4,7,7,512]{3,0,2,1:T(4,128)(2,1)} %param.32) | copy-start | bytes 602116
  2.0 10.2 %copy-start.15 = (s32[4,7,7]{2,0,1:T(4,128)S(1)}, s32[4,7,7]{2,0,1:T(4,128)}, u32[]{:S(2)}) copy-start(s32[4,7,7]{2,0,1:T(4,128)} %param.19) | copy-start | bytes 2356
  2.0 10.2 %copy-start.6 = (f32[1183,16]{0,1:T(8,128)S(1)}, f32[1183,16]{0,1:T(8,128)}, u32[]{:S(2)}) copy-start(f32[1183,16]{0,1:T(8,128)} %param.31) | copy-start | bytes 227140
  2.0 10.2 %copy-start.7 = (s32[4,28,28]{2,0,1:T(4,128)S(1)}, s32[4,28,28]{2,0,1:T(4,128)}, u32[]{:S(2)}) copy-start(s32[4,28,28]{2,0,1:T(4,128)} %param.18) | copy-start | bytes 37636
  2.0 10.2 %copy-start.9 = (f32[1183,4]{0,1:T(4,128)S(1)}, f32[1183,4]{0,1:T(4,128)}, u32[]{:S(2)}) copy-start(f32[1183,4]{0,1:T(4,128)} %param.23) | copy-start | bytes 56788
  2.0 10.2 %copy-start.13 = (bf16[256,1024]{1,0:T(8,128)(2,1)S(1)}, bf16[256,1024]{1,0:T(8,128)(2,1)}, u32[]{:S(2)}) copy-start(bf16[256,1024]{1,0:T(8,128)(2,1)} %constant.2.clone.s_ref) | copy-start | bytes 1572868
  2.3 11.7 %collective-permute-start = (bf16[14,28,2,128]{3,2,1,0:T(2,128)(2,1)S(1)}, bf16[14,28,2,128]{3,2,1,0:T(2,128)(2,1)S(1)}, u32[]{:S(2)}, u32[]{:S(2)}) collective-permute-start(bf16[14,28,2,128]{3,2,1,0:T(2,128)(2,1)S(1)} %bitcast.57), channel_id=1, source_target_pairs={{0,2},{2,0},{1,3},{3,1},{4,6},{6,4},{5,7},{7,5},{8,10},{10,8},{9,1... | collective-permute-start | bytes 602120 | tf_op jit(solution)/shard_map/ppermute | solution.py:872
  5.6 15.3 %collective-permute-start.2 = (bf16[15,28,2,128]{3,2,1,0:T(2,128)(2,1)S(1)}, bf16[15,28,2,128]{3,2,1,0:T(2,128)(2,1)S(1)}, u32[]{:S(2)}, u32[]{:S(2)}) collective-permute-start(bf16[15,28,2,128]{3,2,1,0:T(2,128)(2,1)S(1)} %bitcast.55), channel_id=1, source_target_pairs={{0,2},{2,0},{1,3},{3,1},{4,6},{6,4},{5,7},{7,5},{8,10},{10,8},{9,1... | collective-permute-start | bytes 645128 | tf_op jit(solution)/shard_map/ppermute | solution.py:872
  5.7 15.3 %collective-permute-start.3 = (bf16[2,6,28,128]{3,2,1,0:T(8,128)(2,1)S(1)}, bf16[2,6,28,128]{3,2,1,0:T(8,128)(2,1)S(1)}, u32[]{:S(2)}, u32[]{:S(2)}) collective-permute-start(bf16[2,6,28,128]{3,2,1,0:T(8,128)(2,1)S(1)} %get-tuple-element.73), channel_id=1, source_target_pairs={{0,28},{4,0},{8,4},{12,8},{16,12},{20,16},{24,20},{28,24},{1,29},{... | collective-permute-start | bytes 258056 | tf_op jit(solution)/shard_map/ppermute | solution.py:872
  10.7 10.2 %collective-permute-start.4 = (bf16[2,6,28,128]{3,2,1,0:T(8,128)(2,1)S(1)}, bf16[2,6,28,128]{3,2,1,0:T(8,128)(2,1)S(1)}, u32[]{:S(2)}, u32[]{:S(2)}) collective-permute-start(bf16[2,6,28,128]{3,2,1,0:T(8,128)(2,1)S(1)} %get-tuple-element.74), channel_id=1, source_target_pairs={{0,30},{2,28},{4,2},{6,0},{8,6},{10,4},{12,10},{14,8},{16,14},{18,... | collective-permute-start | bytes 258056 | tf_op jit(solution)/shard_map/ppermute | solution.py:872
  12.2 1.8 %copy-start.5 = (bf16[128,384]{1,0:T(8,128)(2,1)S(1)}, bf16[128,384]{1,0:T(8,128)(2,1)}, u32[]{:S(2)}) copy-start(bf16[128,384]{1,0:T(8,128)(2,1)} %refs_3_.3) | copy-start | bytes 294916
  14.0 3.9 %copy-start = (bf16[512,256]{1,0:T(8,128)(2,1)S(1)}, bf16[512,256]{1,0:T(8,128)(2,1)}, u32[]{:S(2)}) copy-start(bf16[512,256]{1,0:T(8,128)(2,1)} %weight_ref.7) | copy-start | bytes 786436
  14.0 3.9 %copy-start.1 = (f32[512]{0:T(512)S(1)}, f32[512]{0:T(512)}, u32[]{:S(2)}) copy-start(f32[512]{0:T(512)} %param.24) | copy-start | bytes 6148
  18.4 7.1 %collective-permute-start.1 = (bf16[4,5,28,128]{3,2,1,0:T(8,128)(2,1)S(1)}, bf16[4,5,28,128]{3,2,1,0:T(8,128)(2,1)S(1)}, u32[]{:S(2)}, u32[]{:S(2)}) collective-permute-start(bf16[4,5,28,128]{3,2,1,0:T(8,128)(2,1)S(1)} %get-tuple-element.68), channel_id=1, source_target_pairs={{0,28},{4,0},{8,4},{12,8},{16,12},{20,16},{24,20},{28,24},{1,29},{... | collective-permute-start | bytes 430088 | tf_op jit(solution)/shard_map/ppermute | solution.py:872
  20.9 4.6 %copy-start.2 = (bf16[512,1536]{1,0:T(8,128)(2,1)S(1)}, bf16[512,1536]{1,0:T(8,128)(2,1)}, u32[]{:S(2)}) copy-start(bf16[512,1536]{1,0:T(8,128)(2,1)} %p3_ref.1) | copy-start | bytes 4718596
  21.0 4.6 %copy-start.3 = (bf16[1024,512]{1,0:T(8,128)(2,1)S(1)}, bf16[1024,512]{1,0:T(8,128)(2,1)}, u32[]{:S(2)}) copy-start(bf16[1024,512]{1,0:T(8,128)(2,1)} %mw2_ref.1) | copy-start | bytes 3145732
  21.0 4.6 %copy-start.4 = (bf16[512,512]{1,0:T(8,128)(2,1)S(1)}, bf16[512,512]{1,0:T(8,128)(2,1)}, u32[]{:S(2)}) copy-start(bf16[512,512]{1,0:T(8,128)(2,1)} %ow3_ref.1) | copy-start | bytes 1572868
  21.0 4.6 %copy-start.10 = (f32[1024]{0:T(1024)S(1)}, f32[1024]{0:T(1024)}, u32[]{:S(2)}) copy-start(f32[1024]{0:T(1024)} %param.26) | copy-start | bytes 12292
  21.0 4.6 %copy-start.11 = (f32[512]{0:T(512)S(1)}, f32[512]{0:T(512)}, u32[]{:S(2)}) copy-start(f32[512]{0:T(512)} %param.28) | copy-start | bytes 6148
  32.5 9.2 %collective-permute-start.5 = (bf16[4,5,28,128]{3,2,1,0:T(8,128)(2,1)S(1)}, bf16[4,5,28,128]{3,2,1,0:T(8,128)(2,1)S(1)}, u32[]{:S(2)}, u32[]{:S(2)}) collective-permute-start(bf16[4,5,28,128]{3,2,1,0:T(8,128)(2,1)S(1)} %get-tuple-element.83), channel_id=1, source_target_pairs={{0,4},{4,8},{8,12},{12,16},{16,20},{20,24},{24,28},{28,0},{1,5},{5... | collective-permute-start | bytes 430088 | tf_op jit(solution)/shard_map/ppermute | solution.py:872
  39.6 9.3 %collective-permute-start.7 = (bf16[15,28,2,128]{3,2,1,0:T(2,128)(2,1)S(1)}, bf16[15,28,2,128]{3,2,1,0:T(2,128)(2,1)S(1)}, u32[]{:S(2)}, u32[]{:S(2)}) collective-permute-start(bf16[15,28,2,128]{3,2,1,0:T(2,128)(2,1)S(1)} %bitcast.56), channel_id=1, source_target_pairs={{0,2},{2,0},{1,3},{3,1},{4,6},{6,4},{5,7},{7,5},{8,10},{10,8},{9,1... | collective-permute-start | bytes 645128 | tf_op jit(solution)/shard_map/ppermute | solution.py:872
  40.4 8.5 %collective-permute-start.8 = (bf16[4,6,28,128]{3,2,1,0:T(8,128)(2,1)S(1)}, bf16[4,6,28,128]{3,2,1,0:T(8,128)(2,1)S(1)}, u32[]{:S(2)}, u32[]{:S(2)}) collective-permute-start(bf16[4,6,28,128]{3,2,1,0:T(8,128)(2,1)S(1)} %get-tuple-element.110), channel_id=1, source_target_pairs={{0,4},{4,8},{8,12},{12,16},{16,20},{20,24},{24,28},{28,0},{1,5},{5... | collective-permute-start | bytes 516104 | tf_op jit(solution)/shard_map/ppermute | solution.py:872
  47.5 6.8 %collective-permute-start.6 = (bf16[14,28,2,128]{3,2,1,0:T(2,128)(2,1)S(1)}, bf16[14,28,2,128]{3,2,1,0:T(2,128)(2,1)S(1)}, u32[]{:S(2)}, u32[]{:S(2)}) collective-permute-start(bf16[14,28,2,128]{3,2,1,0:T(2,128)(2,1)S(1)} %bitcast.58), channel_id=1, source_target_pairs={{0,2},{2,0},{1,3},{3,1},{4,6},{6,4},{5,7},{7,5},{8,10},{10,8},{9,1... | collective-permute-start | bytes 602120 | tf_op jit(solution)/shard_map/ppermute | solution.py:872
  49.0 5.3 %collective-permute-start.9 = (bf16[2,6,28,128]{3,2,1,0:T(8,128)(2,1)S(1)}, bf16[2,6,28,128]{3,2,1,0:T(8,128)(2,1)S(1)}, u32[]{:S(2)}, u32[]{:S(2)}) collective-permute-start(bf16[2,6,28,128]{3,2,1,0:T(8,128)(2,1)S(1)} %slice.3), channel_id=1, source_target_pairs={{0,2},{2,0},{1,3},{3,1},{4,6},{6,4},{5,7},{7,5},{8,10},{10,8},{9,1... | collective-permute-start | bytes 258056 | tf_op jit(solution)/shard_map/ppermute | solution.py:872
  (2 other events, 3.5 us)
